TPU v7x, 128 devices: a whole 4x4x4 slice. The times are simulated.
128 devices in a mesh: gx: 16 (over x, y), gy: 8 (over z, core).
Axes of the slice: x: 4, y: 4, z: 4, core: 2. Of those that a mesh axis runs over, the one named last changes fastest.
Arguments:
- populations: float32 [19, 256, 32, 1024], P(None, ('gx', 'gy')), may hold values from 0.5 to 1.5
- concentration: float32 [2, 256, 32, 1024], P(None, ('gx', 'gy')), may hold values from 0.5 to 2
- potential: float32 [256, 32, 1024], P(('gx', 'gy')), may hold values from -5.4 to 5.4
- mobility: float32 [256, 32, 1024], P(('gx', 'gy')), may hold values from 0.3 to 1.5
- solid_mask: int32 [256, 32, 1024], P(('gx', 'gy')), may hold values 0 or 1
- block_col: int32 [256], replicated, may hold values from 0 to 31, as said below
Outputs:
- populations_next: float32 [19, 256, 32, 1024], P(None, ('gx', 'gy'))
- concentration_next: float32 [2, 256, 32, 1024], P(None, ('gx', 'gy'))
- potential_next: float32 [256, 32, 1024], P(('gx', 'gy'))
Inputs may be any that keep to these rules, and one draw needn't show every extreme that they name: `block_col`: slot t = ((N i + j) * 2 + k), for device i along gx, j along gy, N devices along gy and k < 2, holds the block of row j at column (2 i + s_j + k) mod 32, where every row j has one start s_j with 0 <= s_j < 2; not all rows have the same start.
All inputs are finite; a program needn't handle non-finite values. No bound on the sum of `solid_mask` on one device may be relied on, other than what follows from the above.
Results may differ from a plain program's by a relative error of at most 0.0003.
Values sent between devices are 32-bit elements; how exact they have to be, the bound alone decides.
A program may use at most 128 MiB of HBM per device.

v0:
```python
import jax
import jax.numpy as jnp
from jax import lax
from jax.sharding import PartitionSpec as P

BS = 32
Q = 19
SPECIES = 2
ITERS = 2
STEPS = 4
BLK_DEV = 2


VELOCITY = (
    (0, 0, 0),
    (1, 0, 0),
    (-1, 0, 0),
    (0, 1, 0),
    (0, -1, 0),
    (0, 0, 1),
    (0, 0, -1),
    (1, 1, 0),
    (-1, -1, 0),
    (1, -1, 0),
    (-1, 1, 0),
    (1, 0, 1),
    (-1, 0, -1),
    (1, 0, -1),
    (-1, 0, 1),
    (0, 1, 1),
    (0, -1, -1),
    (0, 1, -1),
    (0, -1, 1),
)
OPPOSITE = (0, 2, 1, 4, 3, 6, 5, 8, 7, 10, 9, 12, 11, 14, 13, 16, 15, 18, 17)
LATTICE_WEIGHT = (1.0 / 3.0,) + (1.0 / 18.0,) * 6 + (1.0 / 36.0,) * 12
ACROSS_X = (1, 2, 7, 8, 9, 10, 11, 12, 13, 14)
ACROSS_Y = (3, 4, 7, 8, 9, 10, 15, 16, 17, 18)
RELAX_TIME = 0.8
SCREENING = 0.5
APPLIED = 0.4
ION_STEP = 0.05
PECLET = 1.0
FORCE_SCALE = 0.5
VALENCE = (1.0, -1.0)


def with_halo(block, sides, width):
    for axis, dim in sides:
        count = lax.axis_size(axis)
        forward = [(i, i + 1) for i in range(count - 1)]
        forward.append((count - 1, 0))
        backward = [(target, source) for source, target in forward]
        low = lax.ppermute(
            lax.slice_in_dim(block, block.shape[dim] - width, None, axis=dim), axis, forward
        )
        high = lax.ppermute(lax.slice_in_dim(block, 0, width, axis=dim), axis, backward)
        block = jnp.concatenate([low, block, high], axis=dim)
    return block


def row_starts(block_col):
    row_count = lax.axis_size("gy")
    row_here = lax.axis_index("gy")

    def start_of(row_number):
        return lax.dynamic_index_in_dim(block_col, row_number * BLK_DEV, 0, keepdims=False)

    return (
        start_of(row_here),
        start_of((row_here + row_count - 1) % row_count),
        start_of((row_here + 1) % row_count),
    )


def surround(side_part, rim_part, row_start):
    start_here, start_below, start_above = row_start
    channels = rim_part.shape[0]
    extent = rim_part.shape[1]
    with_ends = with_halo(side_part, (("gx", 1),), 1)
    extended = with_halo(rim_part, (("gy", 2),), BS)
    rim_rows = jnp.stack([extended[:, :, :BS], extended[:, :, -BS:]], 0).reshape(
        2, channels, extent * BS
    )
    span_rows = with_halo(rim_rows, (("gx", 2),), extent * BS)
    span_rows = span_rows.reshape(2, channels, 3 * extent, BS)
    lower_rim = lax.dynamic_slice_in_dim(
        span_rows[0], extent + BS * (start_here - start_below) - 1, extent + 2, 1
    )
    upper_rim = lax.dynamic_slice_in_dim(
        span_rows[1], extent + BS * (start_here - start_above) - 1, extent + 2, 1
    )
    return (with_ends, lower_rim, upper_rim)


def assemble(middle, lower_rim, upper_rim):
    return jnp.concatenate([lower_rim, middle, upper_rim], axis=1)


def pad_sides(values):
    return jnp.pad(values, ((1, 1), (0, 0)))


def ghost_scalars(fields, row_start):
    stacked = jnp.stack(fields, 0)
    with_ends, lower_rim, upper_rim = surround(stacked, stacked, row_start)
    return [
        assemble(with_ends[number], lower_rim[number], upper_rim[number])
        for number in range(len(fields))
    ]


def neighbour(padded, own_values, axis_index, toward, depth_index):
    extent, cell_count = own_values.shape
    if axis_index == 0:
        return padded[1 + toward : 1 + toward + extent, BS : BS + cell_count]
    if axis_index == 1:
        return padded[1 : 1 + extent, BS + toward * BS : BS + toward * BS + cell_count]
    if toward > 0:
        shifted = jnp.concatenate([own_values[:, 1:], jnp.zeros_like(own_values[:, :1])], 1)
        return jnp.where(depth_index < BS - 1, shifted, 0.0)
    shifted = jnp.concatenate([jnp.zeros_like(own_values[:, :1]), own_values[:, :-1]], 1)
    return jnp.where(depth_index > 0, shifted, 0.0)


def operate(value_pad, values, transport_pad, transport, diagonal, depth_index):
    result = diagonal * values
    for axis_index in range(3):
        coeff_next = neighbour(transport_pad, transport, axis_index, 1, depth_index)
        value_next = neighbour(value_pad, values, axis_index, 1, depth_index)
        coeff_prev = neighbour(transport_pad, transport, axis_index, -1, depth_index)
        value_prev = neighbour(value_pad, values, axis_index, -1, depth_index)
        result = (
            result
            + transport * coeff_next * (values - value_next)
            - coeff_prev * transport * (value_prev - values)
        )
    return result


def face_flux(coeff_a, coeff_b, conc_a, conc_b, pot_a, pot_b, vel_a, vel_b, valence, applied):
    mean_conc = 0.5 * (conc_a + conc_b)
    potential_drop = pot_b - pot_a - applied
    face_velocity = 0.5 * (vel_a + vel_b)
    return (
        coeff_a
        * coeff_b
        * (
            conc_a
            - conc_b
            - valence * mean_conc * potential_drop
            + PECLET * face_velocity * mean_conc
        )
    )


def body_force(charge, slope_x, slope_y):
    return [
        FORCE_SCALE * charge * (APPLIED - slope_x),
        FORCE_SCALE * charge * (0.0 - slope_y),
        jnp.zeros_like(charge),
    ]


def moments(pop_list):
    density = pop_list[0]
    for pop_index in range(1, len(pop_list)):
        density = density + pop_list[pop_index]
    velocity = []
    for axis_index in range(3):
        momentum = None
        for pop_index in range(len(pop_list)):
            component = VELOCITY[pop_index][axis_index]
            if component != 0:
                signed_pop = pop_list[pop_index] if component > 0 else -pop_list[pop_index]
                momentum = signed_pop if momentum is None else momentum + signed_pop
        velocity.append(momentum / density)
    return (density, velocity)


def collide(pop_list, density, velocity, body_push, fluid_flag):
    shifted = [
        velocity[axis_index] + RELAX_TIME * body_push[axis_index] / density
        for axis_index in range(3)
    ]
    square = shifted[0] * shifted[0] + shifted[1] * shifted[1] + shifted[2] * shifted[2]
    post_list = []
    for pop_index in range(len(pop_list)):
        projection = jnp.zeros_like(density)
        for axis_index in range(3):
            component = VELOCITY[pop_index][axis_index]
            if component > 0:
                projection = projection + shifted[axis_index]
            elif component < 0:
                projection = projection - shifted[axis_index]
        equilibrium = (
            LATTICE_WEIGHT[pop_index]
            * density
            * (1.0 + 3.0 * projection + 4.5 * projection * projection - 1.5 * square)
        )
        relaxed = pop_list[pop_index] - (pop_list[pop_index] - equilibrium) / RELAX_TIME
        post_list.append(jnp.where(fluid_flag, relaxed, pop_list[OPPOSITE[pop_index]]))
    return post_list


def propagate_local(post_list, row_start, depth_index):
    side_part = jnp.stack([post_list[pop_index] for pop_index in ACROSS_X], 0)
    rim_part = jnp.stack([post_list[pop_index] for pop_index in ACROSS_Y], 0)
    with_ends, lower_rim, upper_rim = surround(side_part, rim_part, row_start)
    extent, cell_count = post_list[0].shape
    zero_rim = jnp.zeros((extent + 2, BS), jnp.float32)
    result = []
    for pop_index in range(len(post_list)):
        step_x, step_y, step_z = VELOCITY[pop_index]
        if pop_index in ACROSS_X:
            middle = with_ends[ACROSS_X.index(pop_index)]
        else:
            middle = pad_sides(post_list[pop_index])
        if pop_index in ACROSS_Y:
            slot_y = ACROSS_Y.index(pop_index)
            padded = assemble(middle, lower_rim[slot_y], upper_rim[slot_y])
        else:
            padded = assemble(middle, zero_rim, zero_rim)
        padded = jnp.pad(padded, ((0, 0), (1, 1)))
        start_cell = 1 + BS - step_y * BS - step_z
        shifted = padded[1 - step_x : 1 - step_x + extent, start_cell : start_cell + cell_count]
        inside = (depth_index - step_z >= 0) & (depth_index - step_z < BS)
        result.append(jnp.where(inside, shifted, post_list[OPPOSITE[pop_index]]))
    return result


def global_sum(partial_value):
    return lax.psum(partial_value, ("gx", "gy"))


def local(populations, concentration, potential, mobility, solid_mask, block_col):
    blocks = populations.shape[1]
    extent = blocks * BS
    cell_count = BS * BS
    pop_list = [populations[pop_index].reshape(extent, cell_count) for pop_index in range(Q)]
    ion_conc = [concentration[species].reshape(extent, cell_count) for species in range(SPECIES)]
    phi_field = potential.reshape(extent, cell_count)
    fluid_flag = solid_mask.reshape(extent, cell_count) == 0
    fluid_value = fluid_flag.astype(jnp.float32)
    transport = mobility.reshape(extent, cell_count) * fluid_value
    diagonal = SCREENING * fluid_value + (1.0 - fluid_value)
    depth_index = (jnp.arange(cell_count, dtype=jnp.int32) % BS)[None, :]
    row_start = row_starts(block_col)
    zero_rim = jnp.zeros((extent + 2, BS), jnp.float32)
    transport_pad, phi_pad = ghost_scalars([transport, phi_field], row_start)
    for step_index in range(STEPS):
        density, velocity = moments(pop_list)
        source = fluid_value * (ion_conc[0] - ion_conc[1])
        residual = source - operate(
            phi_pad, phi_field, transport_pad, transport, diagonal, depth_index
        )
        direction = residual
        norm_now = global_sum(jnp.sum(residual * residual))
        for iteration in range(ITERS):
            direction_pad = ghost_scalars([direction], row_start)[0]
            mapped = operate(
                direction_pad, direction, transport_pad, transport, diagonal, depth_index
            )
            step_length = norm_now / global_sum(jnp.sum(direction * mapped))
            phi_field = phi_field + step_length * direction
            residual = residual - step_length * mapped
            if iteration + 1 < ITERS:
                norm_next = global_sum(jnp.sum(residual * residual))
                direction = residual + norm_next / norm_now * direction
                norm_now = norm_next
        side_part = jnp.stack([phi_field, ion_conc[0], ion_conc[1], velocity[0]], 0)
        rim_part = jnp.stack([phi_field, ion_conc[0], ion_conc[1], velocity[1]], 0)
        with_ends, lower_rim, upper_rim = surround(side_part, rim_part, row_start)
        phi_pad = assemble(with_ends[0], lower_rim[0], upper_rim[0])
        ion_pads = [
            assemble(with_ends[1 + species], lower_rim[1 + species], upper_rim[1 + species])
            for species in range(SPECIES)
        ]
        flow_pads = [
            assemble(with_ends[3], zero_rim, zero_rim),
            assemble(pad_sides(velocity[1]), lower_rim[3], upper_rim[3]),
            velocity[2],
        ]
        updated = []
        for species in range(SPECIES):
            divergence = jnp.zeros_like(phi_field)
            conc_now = ion_conc[species]
            for axis_index in range(3):
                applied = APPLIED if axis_index == 0 else 0.0
                forward_term = face_flux(
                    transport,
                    neighbour(transport_pad, transport, axis_index, 1, depth_index),
                    conc_now,
                    neighbour(ion_pads[species], conc_now, axis_index, 1, depth_index),
                    phi_field,
                    neighbour(phi_pad, phi_field, axis_index, 1, depth_index),
                    velocity[axis_index],
                    neighbour(
                        flow_pads[axis_index], velocity[axis_index], axis_index, 1, depth_index
                    ),
                    VALENCE[species],
                    applied,
                )
                backward_term = face_flux(
                    neighbour(transport_pad, transport, axis_index, -1, depth_index),
                    transport,
                    neighbour(ion_pads[species], conc_now, axis_index, -1, depth_index),
                    conc_now,
                    neighbour(phi_pad, phi_field, axis_index, -1, depth_index),
                    phi_field,
                    neighbour(
                        flow_pads[axis_index], velocity[axis_index], axis_index, -1, depth_index
                    ),
                    velocity[axis_index],
                    VALENCE[species],
                    applied,
                )
                divergence = divergence + forward_term - backward_term
            updated.append(conc_now - ION_STEP * divergence)
        ion_conc = updated
        charge = ion_conc[0] - ion_conc[1]
        slope_x = 0.5 * (
            neighbour(phi_pad, phi_field, 0, 1, depth_index)
            - neighbour(phi_pad, phi_field, 0, -1, depth_index)
        )
        slope_y = 0.5 * (
            neighbour(phi_pad, phi_field, 1, 1, depth_index)
            - neighbour(phi_pad, phi_field, 1, -1, depth_index)
        )
        body_push = body_force(charge, slope_x, slope_y)
        post_list = collide(pop_list, density, velocity, body_push, fluid_flag)
        pop_list = propagate_local(post_list, row_start, depth_index)
    pop_out = jnp.stack(pop_list, 0).reshape(Q, blocks, BS, cell_count)
    conc_out = jnp.stack(ion_conc, 0).reshape(SPECIES, blocks, BS, cell_count)
    return (pop_out, conc_out, phi_field.reshape(blocks, BS, cell_count))


def solution(mesh):
    return jax.shard_map(
        local,
        mesh=mesh,
        in_specs=(
            P(None, ("gx", "gy"), None, None),
            P(None, ("gx", "gy"), None, None),
            P(("gx", "gy"), None, None),
            P(("gx", "gy"), None, None),
            P(("gx", "gy"), None, None),
            P(),
        ),
        out_specs=(
            P(None, ("gx", "gy"), None, None),
            P(None, ("gx", "gy"), None, None),
            P(("gx", "gy"), None, None),
        ),
        check_vma=False,
    )
```

profile of v0, /device:TPU:0, one launch (start us, length us, event | category | flops | bytes accessed | tf_op | source)
XLA Modules:
  0.0 1358.9 jit_solution(9562822590427356777)
XLA Ops:
  58.4 64.7 %all-reduce.123 = (f32[]{:T(128)}, f32[]{:T(128)}) all-reduce(f32[]{:T(128)} %get-tuple-element.10, f32[]{:T(128)} %get-tuple-element.9), channel_id=1, replica_groups=mesh['gx'=16,'gy'=8] {'gx','gy'}, use_global_device_ids=true, to_apply=%region_1.2 | all-reduce | flops 2 | bytes 16 | tf_op jit(solution)/shard_map/psum | solution.py:233
  125.2 62.2 %psum.114 = f32[]{:T(128)} all-reduce(f32[]{:T(128)} %multiply_reduce_fusion.9), channel_id=1, replica_groups=mesh['gx'=16,'gy'=8] {'gx','gy'}, use_global_device_ids=true, to_apply=%region_5.6 | all-reduce | flops 1 | bytes 8 | tf_op jit(solution)/shard_map/psum | solution.py:233
  210.5 65.3 %psum.115 = f32[]{:T(128)} all-reduce(f32[]{:T(128)} %fusion.740), channel_id=1, replica_groups=mesh['gx'=16,'gy'=8] {'gx','gy'}, use_global_device_ids=true, to_apply=%region_7.8 | all-reduce | flops 1 | bytes 8 | tf_op jit(solution)/shard_map/psum | solution.py:233
  295.0 6.0 subtract_subtract_fusion.2
  335.5 65.2 %all-reduce.122 = (f32[]{:T(128)}, f32[]{:T(128)}) all-reduce(f32[]{:T(128)} %get-tuple-element.8, f32[]{:T(128)} %get-tuple-element.7), channel_id=1, replica_groups=mesh['gx'=16,'gy'=8] {'gx','gy'}, use_global_device_ids=true, to_apply=%region_9.10 | all-reduce | flops 2 | bytes 16 | tf_op jit(solution)/shard_map/psum | solution.py:233
  402.7 64.6 %psum.118 = f32[]{:T(128)} all-reduce(f32[]{:T(128)} %multiply_reduce_fusion.6), channel_id=1, replica_groups=mesh['gx'=16,'gy'=8] {'gx','gy'}, use_global_device_ids=true, to_apply=%region_13.14 | all-reduce | flops 1 | bytes 8 | tf_op jit(solution)/shard_map/psum | solution.py:233
  473.5 5.6 collective-permute-start.25
  506.3 64.4 %psum.119 = f32[]{:T(128)} all-reduce(f32[]{:T(128)} %fusion.684), channel_id=1, replica_groups=mesh['gx'=16,'gy'=8] {'gx','gy'}, use_global_device_ids=true, to_apply=%region_15.16 | all-reduce | flops 1 | bytes 8 | tf_op jit(solution)/shard_map/psum | solution.py:233
  597.2 5.9 add_divide_fusion.6
  647.4 5.6 collective-permute-start.54
  665.7 65.2 %all-reduce.121 = (f32[]{:T(128)}, f32[]{:T(128)}) all-reduce(f32[]{:T(128)} %get-tuple-element.6, f32[]{:T(128)} %get-tuple-element.5), channel_id=1, replica_groups=mesh['gx'=16,'gy'=8] {'gx','gy'}, use_global_device_ids=true, to_apply=%region_17.18 | all-reduce | flops 2 | bytes 16 | tf_op jit(solution)/shard_map/psum | solution.py:233
  732.9 64.6 %psum.122 = f32[]{:T(128)} all-reduce(f32[]{:T(128)} %multiply_reduce_fusion.3), channel_id=1, replica_groups=mesh['gx'=16,'gy'=8] {'gx','gy'}, use_global_device_ids=true, to_apply=%region_21.22 | all-reduce | flops 1 | bytes 8 | tf_op jit(solution)/shard_map/psum | solution.py:233
  803.7 5.6 collective-permute-start.49
  836.6 64.4 %psum.123 = f32[]{:T(128)} all-reduce(f32[]{:T(128)} %fusion.628), channel_id=1, replica_groups=mesh['gx'=16,'gy'=8] {'gx','gy'}, use_global_device_ids=true, to_apply=%region_23.24 | all-reduce | flops 1 | bytes 8 | tf_op jit(solution)/shard_map/psum | solution.py:233
  927.5 6.1 add_divide_fusion.3
  940.1 5.5 collective-permute-start.66
  976.8 5.5 collective-permute-start.78
  994.9 65.2 %all-reduce.120 = (f32[]{:T(128)}, f32[]{:T(128)}) all-reduce(f32[]{:T(128)} %get-tuple-element.4, f32[]{:T(128)} %get-tuple-element.3), channel_id=1, replica_groups=mesh['gx'=16,'gy'=8] {'gx','gy'}, use_global_device_ids=true, to_apply=%region_25.26 | all-reduce | flops 2 | bytes 16 | tf_op jit(solution)/shard_map/psum | solution.py:233
  1062.0 64.6 %psum.126 = f32[]{:T(128)} all-reduce(f32[]{:T(128)} %multiply_reduce_fusion), channel_id=1, replica_groups=mesh['gx'=16,'gy'=8] {'gx','gy'}, use_global_device_ids=true, to_apply=%region_29.30 | all-reduce | flops 1 | bytes 8 | tf_op jit(solution)/shard_map/psum | solution.py:233
  1132.8 5.6 collective-permute-start.73
  1165.6 64.4 %psum.127 = f32[]{:T(128)} all-reduce(f32[]{:T(128)} %fusion.572), channel_id=1, replica_groups=mesh['gx'=16,'gy'=8] {'gx','gy'}, use_global_device_ids=true, to_apply=%region_31.32 | all-reduce | flops 1 | bytes 8 | tf_op jit(solution)/shard_map/psum | solution.py:233
  1257.8 5.9 add_divide_fusion
  1295.7 5.4 fusion.543
  1312.0 5.7 collective-permute-start.97
  (1197 shorter events, 491.5 us)
Async XLA Ops:
  2.6 26.2 %collective-permute-start.2 = (f32[2,64,32]{2,1,0:T(8,128)S(1)}, f32[2,64,32]{2,1,0:T(8,128)S(1)}, u32[]{:S(2)}, u32[]{:S(2)}) collective-permute-start(f32[2,64,32]{2,1,0:T(8,128)S(1)} %get-tuple-element.447), channel_id=1, source_target_pairs={{0,1},{1,2},{2,3},{3,4},{4,5},{5,6},{6,7},{7,0},{8,9},{9,10},{10,1... | collective-permute-start | bytes 49160 | tf_op jit(solution)/shard_map/ppermute | solution.py:54
  2.6 26.3 %collective-permute-start.3 = (f32[2,64,32]{2,1,0:T(8,128)S(1)}, f32[2,64,32]{2,1,0:T(8,128)S(1)}, u32[]{:S(2)}, u32[]{:S(2)}) collective-permute-start(f32[2,64,32]{2,1,0:T(8,128)S(1)} %get-tuple-element.446), channel_id=1, source_target_pairs={{1,0},{2,1},{3,2},{4,3},{5,4},{6,5},{7,6},{0,7},{9,8},{10,9},{11,1... | collective-permute-start | bytes 49160 | tf_op jit(solution)/shard_map/ppermute | solution.py:57
  7.0 21.7 %collective-permute-start = (f32[2,1,1024]{2,1,0:T(1,128)S(1)}, f32[2,1,1024]{2,1,0:T(1,128)S(1)}, u32[]{:S(2)}, u32[]{:S(2)}) collective-permute-start(f32[2,1,1024]{2,1,0:T(1,128)S(1)} %get-tuple-element.449), channel_id=1, source_target_pairs={{8,0},{16,8},{24,16},{32,24},{40,32},{48,40},{56,48},{64,56},{72,6... | collective-permute-start | bytes 24584 | tf_op jit(solution)/shard_map/ppermute | solution.py:57
  12.2 16.4 %collective-permute-start.1 = (f32[2,1,1024]{2,1,0:T(1,128)S(1)}, f32[2,1,1024]{2,1,0:T(1,128)S(1)}, u32[]{:S(2)}, u32[]{:S(2)}) collective-permute-start(f32[2,1,1024]{2,1,0:T(1,128)S(1)} %get-tuple-element.448), channel_id=1, source_target_pairs={{0,8},{8,16},{16,24},{24,32},{32,40},{40,48},{48,56},{56,64},{64,7... | collective-permute-start | bytes 24584 | tf_op jit(solution)/shard_map/ppermute | solution.py:54
  308.8 13.6 %collective-permute-start.32 = (f32[1,64,32]{2,1,0:T(8,128)S(1)}, f32[1,64,32]{2,1,0:T(8,128)S(1)}, u32[]{:S(2)}, u32[]{:S(2)}) collective-permute-start(f32[1,64,32]{2,1,0:T(8,128)S(1)} %get-tuple-element.561), channel_id=1, source_target_pairs={{0,1},{1,2},{2,3},{3,4},{4,5},{5,6},{6,7},{7,0},{8,9},{9,10},{10,1... | collective-permute-start | bytes 24584 | tf_op jit(solution)/shard_map/ppermute | solution.py:54
  308.8 16.4 %collective-permute-start.33 = (f32[1,64,32]{2,1,0:T(8,128)S(1)}, f32[1,64,32]{2,1,0:T(8,128)S(1)}, u32[]{:S(2)}, u32[]{:S(2)}) collective-permute-start(f32[1,64,32]{2,1,0:T(8,128)S(1)} %get-tuple-element.560), channel_id=1, source_target_pairs={{1,0},{2,1},{3,2},{4,3},{5,4},{6,5},{7,6},{0,7},{9,8},{10,9},{11,1... | collective-permute-start | bytes 24584 | tf_op jit(solution)/shard_map/ppermute | solution.py:57
  314.0 258.0 %collective-permute-start.26 = (f32[10,64,32]{2,1,0:T(8,128)}, f32[10,64,32]{2,1,0:T(8,128)}, u32[]{:S(2)}, u32[]{:S(2)}) collective-permute-start(f32[10,64,32]{2,1,0:T(8,128)} %get-tuple-element.209), channel_id=1, source_target_pairs={{0,1},{1,2},{2,3},{3,4},{4,5},{5,6},{6,7},{7,0},{8,9},{9,10},{10,1... | collective-permute-start | bytes 245768 | tf_op jit(solution)/shard_map/ppermute | solution.py:54
  322.5 250.7 %collective-permute-start.27 = (f32[10,64,32]{2,1,0:T(8,128)}, f32[10,64,32]{2,1,0:T(8,128)}, u32[]{:S(2)}, u32[]{:S(2)}) collective-permute-start(f32[10,64,32]{2,1,0:T(8,128)} %get-tuple-element.208), channel_id=1, source_target_pairs={{1,0},{2,1},{3,2},{4,3},{5,4},{6,5},{7,6},{0,7},{9,8},{10,9},{11,1... | collective-permute-start | bytes 245768 | tf_op jit(solution)/shard_map/ppermute | solution.py:57
  402.7 86.5 %collective-permute-start.24 = (f32[10,1,1024]{2,1,0:T(1,128)}, f32[10,1,1024]{2,1,0:T(1,128)S(1)}, u32[]{:S(2)}, u32[]{:S(2)}) collective-permute-start(f32[10,1,1024]{2,1,0:T(1,128)} %get-tuple-element.211), channel_id=1, source_target_pairs={{0,8},{8,16},{16,24},{24,32},{32,40},{40,48},{48,56},{56,64},{64,7... | collective-permute-start | bytes 122888 | tf_op jit(solution)/shard_map/ppermute | solution.py:54
  473.5 21.1 %collective-permute-start.25 = (f32[10,1,1024]{2,1,0:T(1,128)}, f32[10,1,1024]{2,1,0:T(1,128)S(1)}, u32[]{:S(2)}, u32[]{:S(2)}) collective-permute-start(f32[10,1,1024]{2,1,0:T(1,128)} %get-tuple-element.210), channel_id=1, source_target_pairs={{8,0},{16,8},{24,16},{32,24},{40,32},{48,40},{56,48},{64,56},{72,6... | collective-permute-start | bytes 122888 | tf_op jit(solution)/shard_map/ppermute | solution.py:57
  639.1 13.9 %collective-permute-start.56 = (f32[1,64,32]{2,1,0:T(8,128)S(1)}, f32[1,64,32]{2,1,0:T(8,128)S(1)}, u32[]{:S(2)}, u32[]{:S(2)}) collective-permute-start(f32[1,64,32]{2,1,0:T(8,128)S(1)} %get-tuple-element.533), channel_id=1, source_target_pairs={{0,1},{1,2},{2,3},{3,4},{4,5},{5,6},{6,7},{7,0},{8,9},{9,10},{10,1... | collective-permute-start | bytes 24584 | tf_op jit(solution)/shard_map/ppermute | solution.py:54
  639.1 16.7 %collective-permute-start.57 = (f32[1,64,32]{2,1,0:T(8,128)}, f32[1,64,32]{2,1,0:T(8,128)S(1)}, u32[]{:S(2)}, u32[]{:S(2)}) collective-permute-start(f32[1,64,32]{2,1,0:T(8,128)} %get-tuple-element.532), channel_id=1, source_target_pairs={{1,0},{2,1},{3,2},{4,3},{5,4},{6,5},{7,6},{0,7},{9,8},{10,9},{11,1... | collective-permute-start | bytes 24584 | tf_op jit(solution)/shard_map/ppermute | solution.py:57
  644.3 258.1 %collective-permute-start.50 = (f32[10,64,32]{2,1,0:T(8,128)}, f32[10,64,32]{2,1,0:T(8,128)}, u32[]{:S(2)}, u32[]{:S(2)}) collective-permute-start(f32[10,64,32]{2,1,0:T(8,128)} %get-tuple-element.205), channel_id=1, source_target_pairs={{0,1},{1,2},{2,3},{3,4},{4,5},{5,6},{6,7},{7,0},{8,9},{9,10},{10,1... | collective-permute-start | bytes 245768 | tf_op jit(solution)/shard_map/ppermute | solution.py:54
  653.0 250.6 %collective-permute-start.51 = (f32[10,64,32]{2,1,0:T(8,128)}, f32[10,64,32]{2,1,0:T(8,128)}, u32[]{:S(2)}, u32[]{:S(2)}) collective-permute-start(f32[10,64,32]{2,1,0:T(8,128)} %get-tuple-element.204), channel_id=1, source_target_pairs={{1,0},{2,1},{3,2},{4,3},{5,4},{6,5},{7,6},{0,7},{9,8},{10,9},{11,1... | collective-permute-start | bytes 245768 | tf_op jit(solution)/shard_map/ppermute | solution.py:57
  732.9 86.6 %collective-permute-start.48 = (f32[10,1,1024]{2,1,0:T(1,128)}, f32[10,1,1024]{2,1,0:T(1,128)S(1)}, u32[]{:S(2)}, u32[]{:S(2)}) collective-permute-start(f32[10,1,1024]{2,1,0:T(1,128)} %get-tuple-element.207), channel_id=1, source_target_pairs={{0,8},{8,16},{16,24},{24,32},{32,40},{40,48},{48,56},{56,64},{64,7... | collective-permute-start | bytes 122888 | tf_op jit(solution)/shard_map/ppermute | solution.py:54
  803.7 21.1 %collective-permute-start.49 = (f32[10,1,1024]{2,1,0:T(1,128)}, f32[10,1,1024]{2,1,0:T(1,128)S(1)}, u32[]{:S(2)}, u32[]{:S(2)}) collective-permute-start(f32[10,1,1024]{2,1,0:T(1,128)} %get-tuple-element.206), channel_id=1, source_target_pairs={{8,0},{16,8},{24,16},{32,24},{40,32},{48,40},{56,48},{64,56},{72,6... | collective-permute-start | bytes 122888 | tf_op jit(solution)/shard_map/ppermute | solution.py:57
  968.5 13.8 %collective-permute-start.80 = (f32[1,64,32]{2,1,0:T(8,128)S(1)}, f32[1,64,32]{2,1,0:T(8,128)S(1)}, u32[]{:S(2)}, u32[]{:S(2)}) collective-permute-start(f32[1,64,32]{2,1,0:T(8,128)S(1)} %get-tuple-element.505), channel_id=1, source_target_pairs={{0,1},{1,2},{2,3},{3,4},{4,5},{5,6},{6,7},{7,0},{8,9},{9,10},{10,1... | collective-permute-start | bytes 24584 | tf_op jit(solution)/shard_map/ppermute | solution.py:54
  968.5 16.6 %collective-permute-start.81 = (f32[1,64,32]{2,1,0:T(8,128)}, f32[1,64,32]{2,1,0:T(8,128)S(1)}, u32[]{:S(2)}, u32[]{:S(2)}) collective-permute-start(f32[1,64,32]{2,1,0:T(8,128)} %get-tuple-element.504), channel_id=1, source_target_pairs={{1,0},{2,1},{3,2},{4,3},{5,4},{6,5},{7,6},{0,7},{9,8},{10,9},{11,1... | collective-permute-start | bytes 24584 | tf_op jit(solution)/shard_map/ppermute | solution.py:57
  973.7 257.8 %collective-permute-start.74 = (f32[10,64,32]{2,1,0:T(8,128)}, f32[10,64,32]{2,1,0:T(8,128)}, u32[]{:S(2)}, u32[]{:S(2)}) collective-permute-start(f32[10,64,32]{2,1,0:T(8,128)} %get-tuple-element.201), channel_id=1, source_target_pairs={{0,1},{1,2},{2,3},{3,4},{4,5},{5,6},{6,7},{7,0},{8,9},{9,10},{10,1... | collective-permute-start | bytes 245768 | tf_op jit(solution)/shard_map/ppermute | solution.py:54
  982.3 250.4 %collective-permute-start.75 = (f32[10,64,32]{2,1,0:T(8,128)}, f32[10,64,32]{2,1,0:T(8,128)}, u32[]{:S(2)}, u32[]{:S(2)}) collective-permute-start(f32[10,64,32]{2,1,0:T(8,128)} %get-tuple-element.200), channel_id=1, source_target_pairs={{1,0},{2,1},{3,2},{4,3},{5,4},{6,5},{7,6},{0,7},{9,8},{10,9},{11,1... | collective-permute-start | bytes 245768 | tf_op jit(solution)/shard_map/ppermute | solution.py:57
  1062.0 86.5 %collective-permute-start.72 = (f32[10,1,1024]{2,1,0:T(1,128)}, f32[10,1,1024]{2,1,0:T(1,128)S(1)}, u32[]{:S(2)}, u32[]{:S(2)}) collective-permute-start(f32[10,1,1024]{2,1,0:T(1,128)} %get-tuple-element.203), channel_id=1, source_target_pairs={{0,8},{8,16},{16,24},{24,32},{32,40},{40,48},{48,56},{56,64},{64,7... | collective-permute-start | bytes 122888 | tf_op jit(solution)/shard_map/ppermute | solution.py:54
  1132.8 21.1 %collective-permute-start.73 = (f32[10,1,1024]{2,1,0:T(1,128)}, f32[10,1,1024]{2,1,0:T(1,128)S(1)}, u32[]{:S(2)}, u32[]{:S(2)}) collective-permute-start(f32[10,1,1024]{2,1,0:T(1,128)} %get-tuple-element.202), channel_id=1, source_target_pairs={{8,0},{16,8},{24,16},{32,24},{40,32},{48,40},{56,48},{64,56},{72,6... | collective-permute-start | bytes 122888 | tf_op jit(solution)/shard_map/ppermute | solution.py:57
  1271.2 15.5 %collective-permute-start.90 = (f32[4,1,1024]{2,1,0:T(1,128)}, f32[4,1,1024]{2,1,0:T(1,128)S(1)}, u32[]{:S(2)}, u32[]{:S(2)}) collective-permute-start(f32[4,1,1024]{2,1,0:T(1,128)} %get-tuple-element.320), channel_id=1, source_target_pairs={{8,0},{16,8},{24,16},{32,24},{40,32},{48,40},{56,48},{64,56},{72,6... | collective-permute-start | bytes 49160 | tf_op jit(solution)/shard_map/ppermute | solution.py:57
  1311.9 13.1 collective-permute-start.96
  (373 other events, 2035.9 us)
where the time goes:
time: 1370 us; the launch traced here: 1360 us
  blocking collectives  775 us (57%)
  starting transfers between devices  214 us (16%)
  local copies, waits for them, and re-layouts  184 us (13%)
  other arithmetic  123 us (9%)
  waiting for transfers between devices  39.7 us (3%)
  between operations  24 us (2%)
    psum x12, blocking collectives, global_sum(): return lax.psum(partial_value, ('gx', 'gy'))  775 us
    ppermute x51, starting transfers between devices, with_halo(): lax.ppermute(lax.slice_in_dim(block, 0, width, axis=dim), axis, backward)  210 us
    ppermute x51, waiting for transfers between devices, with_halo(): lax.ppermute(lax.slice_in_dim(block, block.shape[dim] - width, None, axis...  37.4 us
    unnamed x681, local copies, waits for them, and re-layouts  30.8 us
  transfers between devices with their start and end apart: 102, of which 22 were waited for; matrix products, arithmetic and copies ran while one was open for 9% of the time, Pallas kernels for 0%

commit v1 on v0

v1 whole, which is shorter than its diff:
```python
import jax
import jax.numpy as jnp
from jax import lax
from jax.experimental import pallas as pl
from jax.experimental.pallas import tpu as pltpu
from jax.sharding import PartitionSpec as P

BS = 32
Q = 19
STEPS = 4
N_GX = 16
N_GY = 8
N_DEV = N_GX * N_GY
VELOCITY = (
    (0, 0, 0),
    (1, 0, 0),
    (-1, 0, 0),
    (0, 1, 0),
    (0, -1, 0),
    (0, 0, 1),
    (0, 0, -1),
    (1, 1, 0),
    (-1, -1, 0),
    (1, -1, 0),
    (-1, 1, 0),
    (1, 0, 1),
    (-1, 0, -1),
    (1, 0, -1),
    (-1, 0, 1),
    (0, 1, 1),
    (0, -1, -1),
    (0, 1, -1),
    (0, -1, 1),
)
OPPOSITE = (0, 2, 1, 4, 3, 6, 5, 8, 7, 10, 9, 12, 11, 14, 13, 16, 15, 18, 17)
UP_Y = (3, 7, 10, 15, 17)
DOWN_Y = (4, 8, 9, 16, 18)
UP_X = (1, 7, 9, 11, 13)
DOWN_X = (2, 8, 10, 12, 14)
RELAX_TIME = 0.8
SCREENING = 0.5
APPLIED = 0.4
ION_STEP = 0.05
FORCE_SCALE = 0.5

MESH = pl.DeviceIdType.MESH
LANES = 128
TILES = 8
ROWS = 64
EDGE = 16
NR = ROWS + 2 * EDGE
NT = TILES + 2
SIDE = 40
STRIP = ROWS + 2 * SIDE


def tile_offsets():
    hops = lambda a: min(a, 4 - a)
    offs = [
        (a, b, c, d)
        for a in range(4)
        for b in range(4)
        for c in range(4)
        for d in range(2)
        if a + b + c + d
    ]
    offs.sort(key=lambda o: -(hops(o[0]) + hops(o[1]) + hops(o[2]) + 0.1 * o[3]))
    return offs


def kernel(
    col_ref, pop_hbm, conc_hbm, pot_hbm, mob_hbm, mask_hbm,
    pop_out, conc_out, pot_out,
    f, g, phi, r0, w, aw, c, t, kx, ky, kym, kz, kzm, dg, fl, mk,
    ux, uy, uz, rho, rinv, vx, vy, flux,
    ar, sy_r, ry_r, sx_r, rx_r, sy_g, ry_g, sx_g, rx_g, sx_u, ry_u, rx_u,
    in_sem, out_sem, ar_send, ar_recv, send_r, recv_r, send_g, recv_g, send_u, recv_u,
):
    gx = lax.axis_index("gx")
    gy = lax.axis_index("gy")
    right = lax.rem(gx + 1, N_GX)
    left = lax.rem(gx + N_GX - 1, N_GX)
    above = lax.rem(gy + 1, N_GY)
    below = lax.rem(gy + N_GY - 1, N_GY)
    me = gx * N_GY + gy

    lane = lax.broadcasted_iota(jnp.int32, (8, LANES), 1)
    depth = lane % BS
    group = lane // BS
    z_first = depth == 0
    z_last = depth == BS - 1

    def in_copies():
        first = []
        pops = []
        for b in range(2):
            for j in range(TILES):
                lanes = pl.ds(j * LANES, LANES)
                rows = pl.ds(EDGE + b * BS, BS)
                own = pl.ds(b * BS, BS)
                first.append((pot_hbm.at[b, :, lanes], phi.at[1 + j, rows, :], 0))
                first.append((mob_hbm.at[b, :, lanes], t.at[1 + j, rows, :], 0))
                first.append((mask_hbm.at[b, :, lanes], mk.at[j, own, :], 0))
                first.append((conc_hbm.at[:, b, :, lanes], c.at[0, :, 1 + j, rows, :], 0))
                pops.append((pop_hbm.at[:, b, :, lanes], f.at[:, j, own, :], 1))
        return first, pops

    first, pops = in_copies()
    first = [pltpu.make_async_copy(s, d, in_sem.at[0, n]) for n, (s, d, k) in enumerate(first)]
    pops = [pltpu.make_async_copy(s, d, in_sem.at[1, n]) for n, (s, d, k) in enumerate(pops)]
    for copy in first:
        copy.start()
    for copy in pops:
        copy.start()

    barrier = pltpu.get_barrier_semaphore()

    def greet(k, _):
        other = lax.rem(me + k, N_DEV)
        pl.semaphore_signal(
            barrier, inc=1, device_id=(other // N_GY, lax.rem(other, N_GY)), device_id_type=MESH
        )
        return 0

    lax.fori_loop(1, N_DEV, greet, 0)

    def exchange(par, strip_src, strip_dst, x_src, x_dst, send, recv):
        copies = []
        for to_y, dst_side in ((below, 1), (above, 0)):
            src_side = 1 - dst_side
            for to_x, src_row, dst_row, count in (
                (gx, 0, SIDE, ROWS),
                (right, ROWS - SIDE, 0, SIDE),
                (left, 0, SIDE + ROWS, SIDE),
            ):
                copies.append(
                    (
                        strip_src(src_side, src_row, count),
                        strip_dst.at[par, dst_side, :, pl.ds(dst_row, count), :],
                        (to_x, to_y),
                    )
                )
        copies.append((x_src.at[1], x_dst.at[par, 0], (right, gy)))
        copies.append((x_src.at[0], x_dst.at[par, 1], (left, gy)))
        return [
            pltpu.make_async_remote_copy(
                src_ref=s, dst_ref=d, send_sem=send.at[k], recv_sem=recv.at[par, k],
                device_id=dev, device_id_type=MESH,
            )
            for k, (s, d, dev) in enumerate(copies)
        ]

    def staged(ref):
        return lambda side, row, count: ref.at[side, :, pl.ds(row, count), :]

    def ex_r(par):
        return exchange(par, staged(sy_r), ry_r, sx_r, rx_r, send_r, recv_r)

    def ex_g(par):
        return exchange(par, staged(sy_g), ry_g, sx_g, rx_g, send_g, recv_g)

    def ex_u(par):
        def src(side, row, count):
            tile = TILES if side == 1 else 1
            return uy.at[pl.ds(tile, 1), pl.ds(EDGE + row, count), :]

        return exchange(par, src, ry_u, sx_u, rx_u, send_u, recv_u)

    def start(copies):
        for copy in copies:
            copy.start()

    def finish(copies):
        for copy in copies:
            copy.wait()

    here = col_ref[2 * gy]
    ahead = [
        jnp.broadcast_to(here - col_ref[2 * other], (8, LANES)) for other in (below, above)
    ]
    less = [v < 0 for v in ahead]
    more = [v > 0 for v in ahead]

    def strip_rows(ref, par, side, number, k):
        first, same, last = [
            ref[par, side, number, pl.ds(start + 8 * k, 8), :] for start in (0, BS, 2 * BS)
        ]
        return jnp.where(less[side], first, jnp.where(more[side], last, same))

    def own_rows(step):
        return pl.multiple_of(EDGE + 8 * step, 8)

    def rolled(v, shift):
        return pltpu.roll(v, shift % LANES, 1)

    def y_next(v, tile, cache):
        if tile not in cache:
            cache[tile] = rolled(v[tile], -BS)
        if tile + 1 not in v:
            return cache[tile]
        if tile + 1 not in cache:
            cache[tile + 1] = rolled(v[tile + 1], -BS)
        return jnp.where(group < 3, cache[tile], cache[tile + 1])

    def y_prev(v, tile, cache):
        if tile not in cache:
            cache[tile] = rolled(v[tile], BS)
        if tile - 1 not in v:
            return cache[tile]
        if tile - 1 not in cache:
            cache[tile - 1] = rolled(v[tile - 1], BS)
        return jnp.where(group > 0, cache[tile], cache[tile - 1])

    def apply(ref, r, tiles, sink):
        rows = pl.ds(r, 8)
        low = max(0, tiles[0] - 1)
        high = min(NT - 1, tiles[-1] + 1)
        v = {j: ref[j, rows, :] for j in range(low, high + 1)}
        up = {}
        down = {}
        for j in tiles:
            here_v = v[j]
            out = dg[j, rows, :] * here_v
            out = out - kx[j, rows, :] * ref[j, pl.ds(r + 1, 8), :]
            out = out - kx[j, pl.ds(r - 1, 8), :] * ref[j, pl.ds(r - 1, 8), :]
            out = out - ky[j, rows, :] * y_next(v, j, up)
            out = out - kym[j, rows, :] * y_prev(v, j, down)
            out = out - kz[j, rows, :] * rolled(here_v, -1)
            out = out - kzm[j, rows, :] * rolled(here_v, 1)
            sink(j, here_v, out)

    OWN = list(range(1, TILES + 1))
    ALL = list(range(NT))

    def moments(pop):
        p = pop
        xp = p[7] + p[9] + p[11] + p[13] + p[1]
        xm = p[8] + p[10] + p[12] + p[14] + p[2]
        yp = p[15] + p[17] + p[3]
        ym = p[16] + p[18] + p[4]
        density = p[0] + xp + xm + yp + ym + (p[5] + p[6])
        jx = xp - xm
        jy = (yp - ym) + ((p[7] + p[10]) - (p[8] + p[9]))
        jz = (p[5] - p[6]) + ((p[11] + p[14]) - (p[12] + p[13])) + (
            (p[15] + p[18]) - (p[16] + p[17])
        )
        inverse = 1.0 / density
        return density, inverse, jx * inverse, jy * inverse, jz * inverse

    def store_moments(pop, j, r):
        density, inverse, a, b, d = moments(pop)
        rows = pl.ds(r, 8)
        own = pl.ds(pl.multiple_of(r - EDGE, 8), 8)
        rho[j - 1, own, :] = density
        rinv[j - 1, own, :] = inverse
        ux[j, rows, :] = a
        uy[j, rows, :] = b
        uz[j - 1, own, :] = d

    def send_velocity(par):
        for j in OWN:
            sx_u[0, 0, pl.ds(j - 1, 1), :] = ux[j, pl.ds(EDGE, 1), :]
            sx_u[1, 0, pl.ds(j - 1, 1), :] = ux[j, pl.ds(EDGE + ROWS - 1, 1), :]
        start(ex_u(par))

    def take_velocity(par):
        finish(ex_u(par))
        for j in OWN:
            ux[j, pl.ds(EDGE - 1, 1), :] = rx_u[par, 0, 0, pl.ds(j - 1, 1), :]
            ux[j, pl.ds(EDGE + ROWS, 1), :] = rx_u[par, 1, 0, pl.ds(j - 1, 1), :]
        for k in range(10):
            rows = pl.ds(EDGE - 8 + 8 * k, 8)
            uy[0, rows, :] = strip_rows(ry_u, par, 0, 0, k)
            uy[NT - 1, rows, :] = strip_rows(ry_u, par, 1, 0, k)

    def send_residual(par, cp):
        for k in range(8):
            rows = pl.ds(EDGE + 8 * k, 8)
            out = pl.ds(8 * k, 8)
            v = r0[1, rows, :]
            a = rolled(c[cp, 0, 1, rows, :], 2 * BS)
            b = rolled(c[cp, 1, 1, rows, :], 3 * BS)
            sy_r[0, 0, out, :] = jnp.where(group < 2, v, jnp.where(group == 2, a, b))
            v = r0[TILES, rows, :]
            a = rolled(c[cp, 0, TILES, rows, :], BS)
            b = rolled(c[cp, 1, TILES, rows, :], 2 * BS)
            sy_r[1, 0, out, :] = jnp.where(group > 1, v, jnp.where(group == 0, a, b))
        for j in OWN:
            to = pl.ds(j - 1, 1)
            last = EDGE + ROWS - 1
            sx_r[0, 0, to, :] = r0[j, pl.ds(EDGE, 1), :]
            sx_r[0, 1, to, :] = r0[j, pl.ds(EDGE + 1, 1), :]
            sx_r[1, 0, to, :] = r0[j, pl.ds(last, 1), :]
            sx_r[1, 1, to, :] = r0[j, pl.ds(last - 1, 1), :]
            for s in range(2):
                sx_r[0, 2 + s, to, :] = c[cp, s, j, pl.ds(EDGE, 1), :]
                sx_r[1, 2 + s, to, :] = c[cp, s, j, pl.ds(last, 1), :]
        start(ex_r(par))

    def take_residual(par, cp):
        finish(ex_r(par))
        for k in range(10):
            rows = pl.ds(EDGE - 8 + 8 * k, 8)
            v = strip_rows(ry_r, par, 0, 0, k)
            r0[0, rows, :] = v
            c[cp, 0, 0, rows, :] = rolled(v, 3 * BS)
            c[cp, 1, 0, rows, :] = rolled(v, 2 * BS)
            v = strip_rows(ry_r, par, 1, 0, k)
            r0[NT - 1, rows, :] = v
            c[cp, 0, NT - 1, rows, :] = rolled(v, 2 * BS)
            c[cp, 1, NT - 1, rows, :] = rolled(v, BS)
        for j in OWN:
            at = pl.ds(j - 1, 1)
            last = EDGE + ROWS - 1
            r0[j, pl.ds(EDGE - 1, 1), :] = rx_r[par, 0, 0, at, :]
            r0[j, pl.ds(EDGE - 2, 1), :] = rx_r[par, 0, 1, at, :]
            r0[j, pl.ds(last + 1, 1), :] = rx_r[par, 1, 0, at, :]
            r0[j, pl.ds(last + 2, 1), :] = rx_r[par, 1, 1, at, :]
            for s in range(2):
                c[cp, s, j, pl.ds(EDGE - 1, 1), :] = rx_r[par, 0, 2 + s, at, :]
                c[cp, s, j, pl.ds(last + 1, 1), :] = rx_r[par, 1, 2 + s, at, :]

    def send_populations(par):
        for side, tile, names in ((0, 1, DOWN_Y), (1, TILES, UP_Y)):
            home = 0 if side == 0 else 3
            for k in range(8):
                rows = pl.ds(EDGE + 8 * k, 8)
                out = pl.ds(8 * k, 8)
                parts = [
                    rolled(g[q, tile, rows, :], (at % 4 - home) * BS)
                    for at, q in enumerate(names)
                ]
                sy_g[side, 0, out, :] = jnp.where(
                    group == 0, parts[0],
                    jnp.where(group == 1, parts[1], jnp.where(group == 2, parts[2], parts[3])),
                )
                sy_g[side, 1, out, :] = parts[4]
        for side, row, names in ((0, EDGE, DOWN_X), (1, EDGE + ROWS - 1, UP_X)):
            for at, q in enumerate(names):
                for j in OWN:
                    sx_g[side, at, pl.ds(j - 1, 1), :] = g[q, j, pl.ds(row, 1), :]
        start(ex_g(par))

    def take_populations(par):
        finish(ex_g(par))
        for side, tile, names in ((0, 0, UP_Y), (1, NT - 1, DOWN_Y)):
            home = 3 if side == 0 else 0
            for k in range(10):
                rows = pl.ds(EDGE - 8 + 8 * k, 8)
                v = strip_rows(ry_g, par, side, 0, k)
                for at, q in enumerate(names):
                    if at == 4:
                        v = strip_rows(ry_g, par, side, 1, k)
                    g[q, tile, rows, :] = rolled(v, (home - at % 4) * BS)
        for side, row, names in ((0, EDGE - 1, UP_X), (1, EDGE + ROWS, DOWN_X)):
            for at, q in enumerate(names):
                for j in OWN:
                    g[q, j, pl.ds(row, 1), :] = rx_g[par, side, at, pl.ds(j - 1, 1), :]

    def propagate(with_moments):
        @pl.loop(0, 8)
        def _(step):
            r = own_rows(step)
            own = pl.ds(pl.multiple_of(8 * step, 8), 8)

            def pull(q, j):
                return g[q, j, pl.ds(r - VELOCITY[q][0], 8), :]

            caches = {q: {} for q in range(Q)}
            for j in OWN:
                pop = []
                for q in range(Q):
                    _, sy, sz = VELOCITY[q]
                    if sy == 0:
                        v = pull(q, j)
                        if sz:
                            v = rolled(v, sz)
                    else:
                        cache = caches[q]
                        for k in (j, j - sy):
                            if k not in cache:
                                cache[k] = rolled(pull(q, k), sy * BS + sz)
                        if sy > 0:
                            keep = group > 0
                        else:
                            keep = group < 3
                        v = jnp.where(keep, cache[j], cache[j - sy])
                    if sz:
                        wall = z_first if sz > 0 else z_last
                        v = jnp.where(wall, g[OPPOSITE[q], j, pl.ds(r, 8), :], v)
                    f[q, j - 1, own, :] = v
                    pop.append(v)
                if with_moments:
                    store_moments(pop, j, r)

    def collide():
        @pl.loop(0, 8)
        def _(step):
            r = own_rows(step)
            own = pl.ds(pl.multiple_of(8 * step, 8), 8)
            rows = pl.ds(r, 8)
            for j in OWN:
                k = j - 1
                fluid = fl[k, own, :] > 0.0
                density = rho[k, own, :]
                a = vx[k, own, :]
                b = vy[k, own, :]
                d = uz[k, own, :]
                square = a * a + b * b + d * d
                rest = 1.25 - 1.875 * square
                big = density * (1.0 / 18.0)
                small = density * (1.0 / 36.0)
                pop0 = f[0, k, own, :]
                relaxed = density * (1.0 / 3.0) * rest - 0.25 * pop0
                g[0, j, rows, :] = jnp.where(fluid, relaxed, pop0)
                for q in range(1, Q, 2):
                    cx, cy, cz = VELOCITY[q]
                    s = None
                    for comp, val in ((cx, a), (cy, b), (cz, d)):
                        if comp:
                            if s is None:
                                s = val
                            else:
                                s = s + val if comp > 0 else s - val
                    weight = big if q < 7 else small
                    even = weight * (rest + 5.625 * (s * s))
                    odd = weight * (3.75 * s)
                    fa = f[q, k, own, :]
                    fb = f[q + 1, k, own, :]
                    g[q, j, rows, :] = jnp.where(fluid, (even + odd) - 0.25 * fa, fb)
                    g[q + 1, j, rows, :] = jnp.where(fluid, (even - odd) - 0.25 * fb, fa)

    for copy in first:
        copy.wait()

    @pl.loop(0, 8)
    def _(step):
        r = own_rows(step)
        own = pl.ds(pl.multiple_of(8 * step, 8), 8)
        for j in OWN:
            fluid = mk[j - 1, own, :] == 0
            fl[j - 1, own, :] = jnp.where(fluid, 1.0, 0.0)
            t[j, pl.ds(r, 8), :] = jnp.where(fluid, t[j, pl.ds(r, 8), :], -1.0)

    for k in range(8):
        rows = pl.ds(EDGE + 8 * k, 8)
        out = pl.ds(8 * k, 8)
        for side, tile in ((0, 1), (1, TILES)):
            sy_g[side, 0, out, :] = t[tile, rows, :]
            sy_g[side, 1, out, :] = phi[tile, rows, :]
    for j in OWN:
        to = pl.ds(j - 1, 1)
        last = EDGE + ROWS - 1
        sx_g[0, 0, to, :] = t[j, pl.ds(EDGE, 1), :]
        sx_g[0, 1, to, :] = t[j, pl.ds(EDGE + 1, 1), :]
        sx_g[0, 2, to, :] = phi[j, pl.ds(EDGE, 1), :]
        sx_g[1, 0, to, :] = t[j, pl.ds(last, 1), :]
        sx_g[1, 1, to, :] = t[j, pl.ds(last - 1, 1), :]
        sx_g[1, 2, to, :] = phi[j, pl.ds(last, 1), :]
    sx_g[:, 3:5] = jnp.zeros((2, 2, 8, LANES), jnp.float32)
    pl.semaphore_wait(barrier, N_DEV - 1)
    start(ex_g(1))

    for copy in pops:
        copy.wait()

    @pl.loop(0, 8)
    def _(step):
        r = own_rows(step)
        own = pl.ds(pl.multiple_of(8 * step, 8), 8)
        for j in OWN:
            store_moments([f[q, j - 1, own, :] for q in range(Q)], j, r)

    send_velocity(0)

    finish(ex_g(1))
    for k in range(10):
        rows = pl.ds(EDGE - 8 + 8 * k, 8)
        for side, tile in ((0, 0), (1, NT - 1)):
            t[tile, rows, :] = strip_rows(ry_g, 1, side, 0, k)
            phi[tile, rows, :] = strip_rows(ry_g, 1, side, 1, k)
    for j in OWN:
        at = pl.ds(j - 1, 1)
        last = EDGE + ROWS - 1
        t[j, pl.ds(EDGE - 1, 1), :] = rx_g[1, 0, 0, at, :]
        t[j, pl.ds(EDGE - 2, 1), :] = rx_g[1, 0, 1, at, :]
        phi[j, pl.ds(EDGE - 1, 1), :] = rx_g[1, 0, 2, at, :]
        t[j, pl.ds(last + 1, 1), :] = rx_g[1, 1, 0, at, :]
        t[j, pl.ds(last + 2, 1), :] = rx_g[1, 1, 1, at, :]
        phi[j, pl.ds(last + 1, 1), :] = rx_g[1, 1, 2, at, :]

    @pl.loop(0, 10)
    def _(step):
        r = pl.multiple_of(EDGE - 8 + 8 * step, 8)
        rows = pl.ds(r, 8)
        raw = {j: t[j, rows, :] for j in ALL}
        v = {j: jnp.maximum(raw[j], 0.0) for j in ALL}
        up = {}
        down = {}
        for j in ALL:
            fluid = jnp.where(raw[j] >= 0.0, 1.0, 0.0)
            xn = v[j] * jnp.maximum(t[j, pl.ds(r + 1, 8), :], 0.0)
            xp = v[j] * jnp.maximum(t[j, pl.ds(r - 1, 8), :], 0.0)
            yn = v[j] * y_next(v, j, up)
            yp = v[j] * y_prev(v, j, down)
            zn = jnp.where(z_last, 0.0, v[j] * rolled(v[j], -1))
            zp = jnp.where(z_first, 0.0, v[j] * rolled(v[j], 1))
            kx[j, rows, :] = xn
            ky[j, rows, :] = yn
            kym[j, rows, :] = yp
            kz[j, rows, :] = zn
            kzm[j, rows, :] = zp
            diagonal = SCREENING * fluid + (1.0 - fluid)
            dg[j, rows, :] = diagonal + xn + xp + yn + yp + zn + zp

    @pl.loop(0, 8)
    def _(step):
        r = own_rows(step)
        rows = pl.ds(r, 8)
        own = pl.ds(pl.multiple_of(8 * step, 8), 8)

        def sink(j, here_v, out):
            charge = c[0, 0, j, rows, :] - c[0, 1, j, rows, :]
            r0[j, rows, :] = fl[j - 1, own, :] * charge - out

        apply(phi, r, OWN, sink)

    send_residual(0, 0)

    def body(n, tau):
        par = lax.rem(n, 2)
        nxt = 1 - par
        take_residual(par, par)

        def to_w(r, tiles):
            def sink(j, here_v, out):
                w[j, pl.ds(r, 8), :] = out - tau * here_v

            apply(r0, r, tiles, sink)

        @pl.loop(0, 8)
        def _(step):
            to_w(own_rows(step), ALL)

        to_w(EDGE - 8, OWN)
        to_w(EDGE + ROWS, OWN)

        zero = jnp.zeros((8, LANES), jnp.float32)

        def sums(step, acc):
            r = own_rows(step)
            own = pl.ds(pl.multiple_of(8 * step, 8), 8)
            acc = list(acc)

            def sink(j, here_v, out):
                aw[j - 1, own, :] = out
                res = r0[j, pl.ds(r, 8), :]
                acc[0] = acc[0] + res * res
                acc[1] = acc[1] + res * here_v
                acc[2] = acc[2] + here_v * here_v
                acc[3] = acc[3] + here_v * out

            apply(w, r, OWN, sink)
            return tuple(acc)

        acc = lax.fori_loop(0, 8, sums, (zero,) * 4)
        rows4 = []
        for a in acc:
            a = jnp.sum(a, axis=0, keepdims=True)
            a = jnp.broadcast_to(a, (8, LANES))
            a = a + rolled(a, 2 * BS)
            rows4.append(a + rolled(a, BS))
        mine = jnp.where(
            group == 0, rows4[0],
            jnp.where(group == 1, rows4[1], jnp.where(group == 2, rows4[2], rows4[3])),
        )[0:1]
        ar[par, me] = mine
        x4, y4 = gx // 4, lax.rem(gx, 4)
        z4, core = gy // 2, lax.rem(gy, 2)
        for a, b, d, e in tile_offsets():
            dev = (
                lax.rem(x4 + a, 4) * 4 + lax.rem(y4 + b, 4),
                lax.rem(z4 + d, 4) * 2 + lax.rem(core + e, 2),
            )
            pltpu.make_async_remote_copy(
                src_ref=ar.at[par, me], dst_ref=ar.at[par, me],
                send_sem=ar_send, recv_sem=ar_recv.at[par],
                device_id=dev, device_id_type=MESH,
            ).start()

        @pl.when(n > 0)
        def _():
            take_populations(nxt)
            propagate(True)
            send_velocity(par)

        others = ar.at[par, pl.ds(0, N_DEV - 1)]
        pltpu.make_async_copy(others, others, ar_send).wait()
        pltpu.make_async_copy(others, others, ar_recv.at[par]).wait()
        parts = [ar[par, k] for k in range(8)]
        for k in range(8, N_DEV):
            parts[k % 8] = parts[k % 8] + ar[par, k]
        while len(parts) > 1:
            parts = [parts[k] + parts[k + 1] for k in range(0, len(parts), 2)]
        total = parts[0]
        where = lax.broadcasted_iota(jnp.int32, (1, LANES), 1) // BS
        s = [
            jnp.sum(jnp.where(where == k, total, 0.0), axis=1, keepdims=True) for k in range(4)
        ]
        ratio = s[1] / s[0]
        lam = tau + ratio
        first_len = 1.0 / lam
        square = first_len * first_len
        rr1 = square * (s[2] - ratio * ratio * s[0])
        beta = rr1 / s[0]
        curve = square * (
            ratio * ratio * lam * s[0] - 2.0 * ratio * (s[2] + tau * s[1]) + s[3]
        ) - beta * beta * lam * s[0]
        second_len = jnp.where(curve > 0.0, rr1 / jnp.where(curve > 0.0, curve, 1.0), 0.0)
        along_r = first_len + second_len * (first_len * ratio + beta)
        along_w = second_len * first_len
        cr = jnp.broadcast_to(along_r, (8, LANES))
        cw = jnp.broadcast_to(along_w, (8, LANES))
        keep_r = jnp.broadcast_to(1.0 - along_r * tau[0:1, 0:1], (8, LANES))

        def new_phi(r, tiles):
            rows = pl.ds(r, 8)
            for j in tiles:
                phi[j, rows, :] = phi[j, rows, :] + (cr * r0[j, rows, :] - cw * w[j, rows, :])

        @pl.loop(0, 8)
        def _(step):
            new_phi(own_rows(step), ALL)

        new_phi(EDGE - 8, OWN)
        new_phi(EDGE + ROWS, OWN)
        take_velocity(par)

        def faces(k, ca, cb, da, db, pa, pb, ua, ub, half_field):
            hu = 0.25 * (ua + ub)
            hd = 0.5 * (pb - pa)
            if half_field:
                hd = hd - half_field
            return (
                k * ((ca - cb) + (ca + cb) * (hu - hd)),
                k * ((da - db) + (da + db) * (hu + hd)),
            )

        def x_faces(j, r):
            rows = pl.ds(r, 8)
            more = pl.ds(r + 1, 8)
            p_next = phi[j, more, :]
            out = faces(
                kx[j, rows, :],
                c[par, 0, j, rows, :], c[par, 0, j, more, :],
                c[par, 1, j, rows, :], c[par, 1, j, more, :],
                phi[j, rows, :], p_next, ux[j, rows, :], ux[j, more, :], 0.5 * APPLIED,
            )
            flux[0, j - 1, rows, :] = out[0]
            flux[1, j - 1, rows, :] = out[1]
            return out, p_next

        for j in OWN:
            x_faces(j, EDGE - 8)

        @pl.loop(0, 8)
        def _(step):
            r = own_rows(step)
            rows = pl.ds(r, 8)
            less = pl.ds(r - 1, 8)
            own = pl.ds(pl.multiple_of(8 * step, 8), 8)
            p = {j: phi[j, rows, :] for j in ALL}
            a = {j: c[par, 0, j, rows, :] for j in ALL}
            b = {j: c[par, 1, j, rows, :] for j in ALL}
            v = {j: uy[j, rows, :] for j in ALL}
            pc, ac, bc, vc, pm = {}, {}, {}, {}, {}
            y0 = {}
            y1 = {}
            for j in range(NT - 1):
                pn = y_next(p, j, pc)
                y0[j], y1[j] = faces(
                    ky[j, rows, :], a[j], y_next(a, j, ac), b[j], y_next(b, j, bc),
                    p[j], pn, v[j], y_next(v, j, vc), 0.0,
                )
                if j == 0:
                    continue
                (x0, x1), p_next = x_faces(j, r)
                d0 = x0 - flux[0, j - 1, less, :]
                d1 = x1 - flux[1, j - 1, less, :]
                if j == 1:
                    y0c, y1c = {}, {}
                d0 = d0 + y0[j] - y_prev(y0, j, y0c)
                d1 = d1 + y1[j] - y_prev(y1, j, y1c)
                vz = uz[j - 1, own, :]
                z0, z1 = faces(
                    kz[j, rows, :], a[j], rolled(a[j], -1), b[j], rolled(b[j], -1),
                    p[j], rolled(p[j], -1), vz, rolled(vz, -1), 0.0,
                )
                d0 = d0 + z0 - rolled(z0, 1)
                d1 = d1 + z1 - rolled(z1, 1)
                new0 = a[j] - ION_STEP * d0
                new1 = b[j] - ION_STEP * d1
                c[nxt, 0, j, rows, :] = new0
                c[nxt, 1, j, rows, :] = new1
                charge = new0 - new1
                push = (FORCE_SCALE * RELAX_TIME) * charge * rinv[j - 1, own, :]
                vx[j - 1, own, :] = ux[j, rows, :] + push * (
                    APPLIED - 0.5 * (p_next - phi[j, less, :])
                )
                vy[j - 1, own, :] = v[j] - push * (0.5 * (pn - y_prev(p, j, pm)))
                r0[j, rows, :] = (
                    keep_r * r0[j, rows, :] - cr * w[j, rows, :] + cw * aw[j - 1, own, :]
                    + fl[j - 1, own, :] * (charge - (a[j] - b[j]))
                )

        @pl.when(n < STEPS - 1)
        def _():
            send_residual(nxt, nxt)

        collide()
        send_populations(par)
        return jnp.broadcast_to(lam, (8, LANES))

    lax.fori_loop(0, STEPS, body, jnp.ones((8, LANES), jnp.float32))

    done = []
    for b in range(2):
        for j in range(TILES):
            lanes = pl.ds(j * LANES, LANES)
            rows = pl.ds(EDGE + b * BS, BS)
            done.append((phi.at[1 + j, rows, :], pot_out.at[b, :, lanes]))
            done.append((c.at[0, :, 1 + j, rows, :], conc_out.at[:, b, :, lanes]))
    done = [pltpu.make_async_copy(s, d, out_sem.at[0, n]) for n, (s, d) in enumerate(done)]
    for copy in done:
        copy.start()
    take_populations((STEPS - 1) % 2)
    propagate(False)
    last = []
    for b in range(2):
        for j in range(TILES):
            lanes = pl.ds(j * LANES, LANES)
            last.append(
                pltpu.make_async_copy(
                    f.at[:, j, pl.ds(b * BS, BS), :],
                    pop_out.at[:, b, :, lanes],
                    out_sem.at[1, b * TILES + j],
                )
            )
    for copy in last:
        copy.start()
    for copy in done + last:
        copy.wait()


def local(populations, concentration, potential, mobility, solid_mask, block_col):
    blocks = populations.shape[1]
    anywhere = pl.BlockSpec(memory_space=pl.ANY)
    f32 = jnp.float32

    def field(*lead):
        return pltpu.VMEM(lead + (NT, NR, LANES), f32)

    def bare(*lead):
        return pltpu.VMEM(lead + (TILES, ROWS, LANES), f32)

    def vm(*shape):
        return pltpu.VMEM(shape + (LANES,), f32)

    scratch = [
        bare(Q), field(Q), field(), field(), field(), bare(), field(2, 2), field(),
        field(), field(), field(), field(), field(), field(), bare(),
        pltpu.VMEM((TILES, ROWS, LANES), jnp.int32),
        field(), field(), bare(), bare(), bare(), bare(), bare(),
        pltpu.VMEM((2, TILES, NR, LANES), f32),
        vm(2, N_DEV, 1),
        vm(2, 1, ROWS), vm(2, 2, 1, STRIP), vm(2, 4, 8), vm(2, 2, 4, 8),
        vm(2, 2, ROWS), vm(2, 2, 2, STRIP), vm(2, 5, 8), vm(2, 2, 5, 8),
        vm(2, 1, 8), vm(2, 2, 1, STRIP), vm(2, 2, 1, 8),
        pltpu.SemaphoreType.DMA((2, 64)),
        pltpu.SemaphoreType.DMA((2, 32)),
        pltpu.SemaphoreType.DMA,
        pltpu.SemaphoreType.DMA((2,)),
        pltpu.SemaphoreType.DMA((8,)), pltpu.SemaphoreType.DMA((2, 8)),
        pltpu.SemaphoreType.DMA((8,)), pltpu.SemaphoreType.DMA((2, 8)),
        pltpu.SemaphoreType.DMA((8,)), pltpu.SemaphoreType.DMA((2, 8)),
    ]
    return pl.pallas_call(
        kernel,
        out_shape=(
            jax.ShapeDtypeStruct(populations.shape, f32),
            jax.ShapeDtypeStruct(concentration.shape, f32),
            jax.ShapeDtypeStruct(potential.shape, f32),
        ),
        in_specs=[pl.BlockSpec(memory_space=pltpu.SMEM)] + [anywhere] * 5,
        out_specs=(anywhere,) * 3,
        scratch_shapes=scratch,
        compiler_params=pltpu.CompilerParams(
            collective_id=0, has_side_effects=True, vmem_limit_bytes=48 * 1024 * 1024
        ),
        cost_estimate=pl.CostEstimate(
            flops=100_000_000, bytes_accessed=12_000_000, transcendentals=0
        ),
    )(block_col, populations, concentration, potential, mobility, solid_mask)


def solution(mesh):
    split = ("gx", "gy")
    return jax.shard_map(
        local,
        mesh=mesh,
        in_specs=(
            P(None, split, None, None),
            P(None, split, None, None),
            P(split, None, None),
            P(split, None, None),
            P(split, None, None),
            P(),
        ),
        out_specs=(P(None, split, None, None), P(None, split, None, None), P(split, None, None)),
        check_vma=False,
    )
```

time: 1370 us -> 120 us (0.09)
  blocking collectives: 775 us -> 0 us
  starting transfers between devices: 214 us -> 0 us
  local copies, waits for them, and re-layouts: 184 us -> 11.5 us
  other arithmetic: 123 us -> 0 us
  Pallas kernels: 0 us -> 107 us
  waiting for transfers between devices: 39.7 us -> 0 us
  between operations: 24 us -> 0.65 us
    psum x12 -> x0, blocking collectives: 775 us -> none  [global_sum(): return lax.psum(partial_value, ('gx', 'gy'))]
    ppermute x102 -> x0, starting transfers between devices: 214 us -> none  [the longest x51 210 us: with_halo(): lax.ppermute(lax.slice_in_dim(block, 0, width, axis=dim), axis, backward)]
    pallas_call x0 -> x1, Pallas kernels: none -> 107 us  [local(): pl.pallas_call(kernel, out_shape=(jax.ShapeDtypeStruct(populations.shape,...]
    squeeze x68 -> x0, local copies, waits for them, and re-layouts: 57.5 us -> none  [the longest x17 16.1 us: surround(): span_rows[1]]
    slice x76 -> x0, local copies, waits for them, and re-layouts: 43.4 us -> none  [the longest x21 18.7 us: neighbour(): own_values[:, 1:]]
    ppermute x102 -> x0, waiting for transfers between devices: 39.7 us -> none  [the longest x51 37.4 us: with_halo(): lax.ppermute(lax.slice_in_dim(block, block.shape[dim] - width, None, axis...]
    another operation x60 -> x0, local copies, waits for them, and re-layouts: 27.4 us -> none  [the longest x51 26.5 us: surround(): jnp.stack([extended[:, :, :BS], extended[:, :, -BS:]], 0)]
    select_n x16 -> x0, other arithmetic: 26.4 us -> none  [the longest x11 17.6 us: collide(): jnp.where(fluid_flag, relaxed, pop_list[OPPOSITE[pop_index]])]
  transfers between devices with their start and end apart: 102 -> 0, of which waited for: 22 -> 0; matrix products, arithmetic and copies ran while one was open for 9% -> 0% of each run, Pallas kernels for 0% -> 0%
where the time goes in v1:
time: 120 us
  Pallas kernels  107 us (89%)
  local copies, waits for them, and re-layouts  11.5 us (10%)
    pallas_call x1, Pallas kernels, local(): pl.pallas_call(kernel, out_shape=(jax.ShapeDtypeStruct(populations.shape,...  107 us
    unnamed x13, local copies, waits for them, and re-layouts  11.5 us

profile of v1, /device:TPU:0, one launch (start us, length us, event | category | flops | bytes accessed | tf_op | source)
XLA Modules:
  0.0 119.6 jit_solution(530682641021393994)
XLA Ops:
  0.6 0.0 copy-start
  0.6 1.0 copy-done
  1.7 0.0 copy-start.1
  1.7 0.9 copy-done.1
  2.6 0.0 copy-start.2
  2.6 0.9 copy-done.2
  3.6 0.0 copy-start.3
  3.6 0.9 copy-done.3
  4.5 0.0 copy-start.4
  4.5 0.7 copy-done.4
  5.2 107.4 %shard_map.85 = (f32[19,2,32,1024]{3,2,1,0:T(8,128)}, f32[2,2,32,1024]{3,2,1,0:T(8,128)S(1)}, f32[2,32,1024]{2,1,0:T(8,128)S(1)}) custom-call(s32[256]{0:T(256)S(1)} %copy-done.4, f32[19,2,32,1024]{3,2,1,0:T(8,128)} %pop_hbm.1, f32[2,2,32,1024]{3,2,1,0:T(8,128)S(1)} %copy-done, f32[2,32,1024]{2,1,0:T(8,128)S(1)} %copy-done.1, f32[2,32,1024]{2,1,0:T(8,128)S(1)} %copy-done.2, ...), custom_call_target="tpu_custom_call" | custom-call | flops 100000000 | bytes 12000000 | tf_op jit(solution)/shard_map/pallas_call | solution.py:787
  112.6 5.5 %copy.12 = f32[19,2,32,1024]{3,2,1,0:T(8,128)} copy(f32[19,2,32,1024]{3,2,1,0:T(8,128)} %get-tuple-element.6) | data formatting | bytes 9961472
  118.1 0.8 copy.13
  118.9 0.7 copy.14
Async XLA Ops:
  0.6 1.0 copy-start
  1.7 0.9 copy-start.1
  2.6 0.9 copy-start.2
  3.6 0.9 copy-start.3
  4.5 0.7 copy-start.4

commit v2 on v1

v2 whole, which is shorter than its diff:
```python
import jax
import jax.numpy as jnp
from jax import lax
from jax.experimental import pallas as pl
from jax.experimental.pallas import tpu as pltpu
from jax.sharding import PartitionSpec as P

BS = 32
Q = 19
STEPS = 4
N_GX = 16
N_GY = 8
N_DEV = N_GX * N_GY
VELOCITY = (
    (0, 0, 0),
    (1, 0, 0),
    (-1, 0, 0),
    (0, 1, 0),
    (0, -1, 0),
    (0, 0, 1),
    (0, 0, -1),
    (1, 1, 0),
    (-1, -1, 0),
    (1, -1, 0),
    (-1, 1, 0),
    (1, 0, 1),
    (-1, 0, -1),
    (1, 0, -1),
    (-1, 0, 1),
    (0, 1, 1),
    (0, -1, -1),
    (0, 1, -1),
    (0, -1, 1),
)
OPPOSITE = (0, 2, 1, 4, 3, 6, 5, 8, 7, 10, 9, 12, 11, 14, 13, 16, 15, 18, 17)
UP_Y = (3, 7, 10, 15, 17)
DOWN_Y = (4, 8, 9, 16, 18)
UP_X = (1, 7, 9, 11, 13)
DOWN_X = (2, 8, 10, 12, 14)
RELAX_TIME = 0.8
SCREENING = 0.5
APPLIED = 0.4
ION_STEP = 0.05
FORCE_SCALE = 0.5

MESH = pl.DeviceIdType.MESH
LANES = 128
TILES = 8
ROWS = 64
EDGE = 16
NR = ROWS + 2 * EDGE
NT = TILES + 2
VMEM_LIMIT = 60 * 1024 * 1024
UNROLL_APPLY = 4
UNROLL_XFLUX = 1
UNROLL_BORDER = 2
UNROLL_INSIDE = 2
UNROLL_LBM = 2
SIDE = 40
STRIP = ROWS + 2 * SIDE


def tile_offsets():
    hops = lambda a: min(a, 4 - a)
    offs = [
        (a, b, c, d)
        for a in range(4)
        for b in range(4)
        for c in range(4)
        for d in range(2)
        if a + b + c + d
    ]
    offs.sort(key=lambda o: -(hops(o[0]) + hops(o[1]) + hops(o[2]) + 0.1 * o[3]))
    return offs


def stream(g, f, r, own, tiles, sink):
    lane = lax.broadcasted_iota(jnp.int32, (8, LANES), 1)
    depth = lane % BS
    group = lane // BS

    def pull(q, j):
        return g[q, j, pl.ds(r - VELOCITY[q][0], 8), :]

    caches = {q: {} for q in range(Q)}
    for j in tiles:
        pop = []
        for q in range(Q):
            _, sy, sz = VELOCITY[q]
            if sy == 0:
                v = pull(q, j)
                if sz:
                    v = pltpu.roll(v, sz % LANES, 1)
            else:
                cache = caches[q]
                for k in (j, j - sy):
                    if k not in cache:
                        cache[k] = pltpu.roll(pull(q, k), (sy * BS + sz) % LANES, 1)
                v = jnp.where(group > 0 if sy > 0 else group < 3, cache[j], cache[j - sy])
            if sz:
                wall = depth == (0 if sz > 0 else BS - 1)
                v = jnp.where(wall, g[OPPOSITE[q], j, pl.ds(r, 8), :], v)
            f[q, own, (j - 1) * LANES : j * LANES] = v
            pop.append(v)
        if sink is not None:
            sink(pop, j)


def kernel(
    col_ref, pop_hbm, conc_hbm, pot_hbm, mob_hbm, mask_hbm,
    g_out, conc_out, pot_out,
    f, g, phi, r0, w, aw, c0, c1, n0, n1, t, kx, ky, kym, kz, kzm, dg, fl, mk,
    ux, uy, uz, rho, rinv, vx, vy, flux0, flux1, dy0, dy1, dz0, dz1, slope, r_next,
    ar, sy_r, ry_r, sx_r, rx_r, sy_g, ry_g, sx_g, rx_g, sx_u, ry_u, rx_u, sy_i, ry_i, sx_i, rx_i,
    in_sem, out_sem, ar_send, ar_recv, send_r, recv_r, send_g, recv_g, send_u, recv_u,
    send_i, recv_i,
):
    gx = lax.axis_index("gx")
    gy = lax.axis_index("gy")
    right = lax.rem(gx + 1, N_GX)
    left = lax.rem(gx + N_GX - 1, N_GX)
    above = lax.rem(gy + 1, N_GY)
    below = lax.rem(gy + N_GY - 1, N_GY)
    me = gx * N_GY + gy

    lane = lax.broadcasted_iota(jnp.int32, (8, LANES), 1)
    depth = lane % BS
    group = lane // BS
    z_first = depth == 0
    z_last = depth == BS - 1

    loads = []
    for j in range(TILES):
        lanes = pl.ds(j * LANES, LANES)
        rows = pl.ds(EDGE, ROWS)
        loads.append((mob_hbm.at[:, lanes], t.at[1 + j, rows, :]))
        loads.append((mask_hbm.at[:, lanes], mk.at[j]))
        loads.append((pot_hbm.at[:, lanes], phi.at[1 + j, rows, :]))
        loads.append((conc_hbm.at[0, :, lanes], c0.at[1 + j, rows, :]))
        loads.append((conc_hbm.at[1, :, lanes], c1.at[1 + j, rows, :]))
    first = [pltpu.make_async_copy(s, d, in_sem.at[n]) for n, (s, d) in enumerate(loads)]
    pops = [pltpu.make_async_copy(pop_hbm, f, in_sem.at[len(first)])]
    for copy in first:
        copy.start()
    for copy in pops:
        copy.start()

    barrier = pltpu.get_barrier_semaphore()

    def greet(k, _):
        other = lax.rem(me + k, N_DEV)
        pl.semaphore_signal(
            barrier, inc=1, device_id=(other // N_GY, lax.rem(other, N_GY)), device_id_type=MESH
        )
        return 0

    lax.fori_loop(1, N_DEV, greet, 0)

    def exchange(par, strip_src, strip_dst, x_src, x_dst, send, recv):
        copies = []
        for to_y, dst_side in ((below, 1), (above, 0)):
            src_side = 1 - dst_side
            for to_x, src_row, dst_row, count in (
                (gx, 0, SIDE, ROWS),
                (right, ROWS - SIDE, 0, SIDE),
                (left, 0, SIDE + ROWS, SIDE),
            ):
                copies.append(
                    (
                        strip_src(src_side, src_row, count),
                        strip_dst.at[par, dst_side, :, pl.ds(dst_row, count), :],
                        (to_x, to_y),
                    )
                )
        copies.append((x_src.at[1], x_dst.at[par, 0], (right, gy)))
        copies.append((x_src.at[0], x_dst.at[par, 1], (left, gy)))
        return [
            pltpu.make_async_remote_copy(
                src_ref=s, dst_ref=d, send_sem=send.at[k], recv_sem=recv.at[par, k],
                device_id=dev, device_id_type=MESH,
            )
            for k, (s, d, dev) in enumerate(copies)
        ]

    def staged(ref):
        return lambda side, row, count: ref.at[side, :, pl.ds(row, count), :]

    def ex_r(par):
        return exchange(par, staged(sy_r), ry_r, sx_r, rx_r, send_r, recv_r)

    def ex_g(par):
        return exchange(par, staged(sy_g), ry_g, sx_g, rx_g, send_g, recv_g)

    def ex_u(par):
        def src(side, row, count):
            tile = TILES if side == 1 else 1
            return uy.at[pl.ds(tile, 1), pl.ds(EDGE + row, count), :]

        return exchange(par, src, ry_u, sx_u, rx_u, send_u, recv_u)

    def start(copies):
        for copy in copies:
            copy.start()

    def finish(copies):
        for copy in copies:
            copy.wait()

    here = col_ref[2 * gy]
    ahead = [
        jnp.broadcast_to(here - col_ref[2 * other], (8, LANES)) for other in (below, above)
    ]
    less = [v < 0 for v in ahead]
    more = [v > 0 for v in ahead]

    def strip_rows(ref, par, side, number, k):
        first, same, last = [
            ref[par, side, number, pl.ds(start + 8 * k, 8), :] for start in (0, BS, 2 * BS)
        ]
        return jnp.where(less[side], first, jnp.where(more[side], last, same))

    def own_rows(step):
        return pl.multiple_of(EDGE + 8 * step, 8)

    def rolled(v, shift):
        return pltpu.roll(v, shift % LANES, 1)

    def y_next(load, tile, cache, top=NT - 1):
        for k in (tile, min(tile + 1, top)):
            if k not in cache:
                cache[k] = rolled(load(k), -BS)
        if tile == top:
            return cache[tile]
        return jnp.where(group < 3, cache[tile], cache[tile + 1])

    def y_prev(load, tile, cache, bottom=0):
        for k in (max(tile - 1, bottom), tile):
            if k not in cache:
                cache[k] = rolled(load(k), BS)
        if tile == bottom:
            return cache[tile]
        return jnp.where(group > 0, cache[tile], cache[tile - 1])

    def loader(ref, rows):
        return lambda j: ref[j, rows, :]

    def apply(ref, r, tiles, sink):
        rows = pl.ds(r, 8)
        load = loader(ref, rows)
        up = {}
        down = {}
        for j in tiles:
            here_v = load(j)
            out = dg[j, rows, :] * here_v
            out = out - kx[j, rows, :] * ref[j, pl.ds(r + 1, 8), :]
            out = out - kx[j, pl.ds(r - 1, 8), :] * ref[j, pl.ds(r - 1, 8), :]
            out = out - ky[j, rows, :] * y_next(load, j, up)
            out = out - kym[j, rows, :] * y_prev(load, j, down)
            out = out - kz[j, rows, :] * rolled(here_v, -1)
            out = out - kzm[j, rows, :] * rolled(here_v, 1)
            sink(j, here_v, out)

    OWN = list(range(1, TILES + 1))
    ALL = list(range(NT))

    def border(work):
        @pl.loop(0, 2, unroll=True)
        def _(k):
            work(7 * k, OWN)

        @pl.loop(1, 7, unroll=UNROLL_BORDER)
        def _(step):
            work(step, OWN[:1])
            work(step, OWN[-1:])

    def inside(work):
        @pl.loop(1, 7, unroll=UNROLL_INSIDE)
        def _(step):
            work(step, OWN[1:-1])

    def moments(pop):
        p = pop
        xp = p[7] + p[9] + p[11] + p[13] + p[1]
        xm = p[8] + p[10] + p[12] + p[14] + p[2]
        yp = p[15] + p[17] + p[3]
        ym = p[16] + p[18] + p[4]
        density = p[0] + xp + xm + yp + ym + (p[5] + p[6])
        jx = xp - xm
        jy = (yp - ym) + ((p[7] + p[10]) - (p[8] + p[9]))
        jz = (p[5] - p[6]) + ((p[11] + p[14]) - (p[12] + p[13])) + (
            (p[15] + p[18]) - (p[16] + p[17])
        )
        inverse = 1.0 / density
        return density, inverse, jx * inverse, jy * inverse, jz * inverse

    def store_moments(pop, j, r):
        density, inverse, a, b, d = moments(pop)
        rows = pl.ds(r, 8)
        own = pl.ds(pl.multiple_of(r - EDGE, 8), 8)
        rho[j - 1, own, :] = density
        rinv[j - 1, own, :] = inverse
        ux[j, rows, :] = a
        uy[j, rows, :] = b
        uz[j - 1, own, :] = d

    def send_velocity(par):
        for j in OWN:
            sx_u[0, 0, pl.ds(j - 1, 1), :] = ux[j, pl.ds(EDGE, 1), :]
            sx_u[1, 0, pl.ds(j - 1, 1), :] = ux[j, pl.ds(EDGE + ROWS - 1, 1), :]
        start(ex_u(par))

    def take_velocity(par):
        finish(ex_u(par))
        for j in OWN:
            ux[j, pl.ds(EDGE - 1, 1), :] = rx_u[par, 0, 0, pl.ds(j - 1, 1), :]
            ux[j, pl.ds(EDGE + ROWS, 1), :] = rx_u[par, 1, 0, pl.ds(j - 1, 1), :]
        for k in range(10):
            rows = pl.ds(EDGE - 8 + 8 * k, 8)
            uy[0, rows, :] = strip_rows(ry_u, par, 0, 0, k)
            uy[NT - 1, rows, :] = strip_rows(ry_u, par, 1, 0, k)

    def send_residual(par):
        for k in range(8):
            out = pl.ds(8 * k, 8)
            a = rolled(n0[0, out, :], 2 * BS)
            b = rolled(n1[0, out, :], 3 * BS)
            sy_r[0, 0, out, :] = jnp.where(
                group < 2, r_next[0, out, :], jnp.where(group == 2, a, b)
            )
            a = rolled(n0[TILES - 1, out, :], BS)
            b = rolled(n1[TILES - 1, out, :], 2 * BS)
            sy_r[1, 0, out, :] = jnp.where(
                group > 1, r_next[TILES - 1, out, :], jnp.where(group == 0, a, b)
            )
        for k in range(TILES):
            to = pl.ds(k, 1)
            for side, row, ahead in ((0, 0, 1), (1, ROWS - 1, -1)):
                sx_r[side, 0, to, :] = r_next[k, pl.ds(row, 1), :]
                sx_r[side, 1, to, :] = r_next[k, pl.ds(row + ahead, 1), :]
                sx_r[side, 2, to, :] = n0[k, pl.ds(row, 1), :]
                sx_r[side, 3, to, :] = n1[k, pl.ds(row, 1), :]
        start(ex_r(par))

    def take_residual(par):
        finish(ex_r(par))
        for k in range(10):
            rows = pl.ds(EDGE - 8 + 8 * k, 8)
            v = strip_rows(ry_r, par, 0, 0, k)
            r0[0, rows, :] = v
            c0[0, rows, :] = rolled(v, 3 * BS)
            c1[0, rows, :] = rolled(v, 2 * BS)
            v = strip_rows(ry_r, par, 1, 0, k)
            r0[NT - 1, rows, :] = v
            c0[NT - 1, rows, :] = rolled(v, 2 * BS)
            c1[NT - 1, rows, :] = rolled(v, BS)
        for j in OWN:
            at = pl.ds(j - 1, 1)
            last = EDGE + ROWS - 1
            r0[j, pl.ds(EDGE - 1, 1), :] = rx_r[par, 0, 0, at, :]
            r0[j, pl.ds(EDGE - 2, 1), :] = rx_r[par, 0, 1, at, :]
            r0[j, pl.ds(last + 1, 1), :] = rx_r[par, 1, 0, at, :]
            r0[j, pl.ds(last + 2, 1), :] = rx_r[par, 1, 1, at, :]
            for s, ref in enumerate((c0, c1)):
                ref[j, pl.ds(EDGE - 1, 1), :] = rx_r[par, 0, 2 + s, at, :]
                ref[j, pl.ds(last + 1, 1), :] = rx_r[par, 1, 2 + s, at, :]

    def send_populations(par):
        for side, tile, names in ((0, 1, DOWN_Y), (1, TILES, UP_Y)):
            home = 0 if side == 0 else 3
            for k in range(8):
                rows = pl.ds(EDGE + 8 * k, 8)
                out = pl.ds(8 * k, 8)
                parts = [
                    rolled(g[q, tile, rows, :], (at % 4 - home) * BS)
                    for at, q in enumerate(names)
                ]
                sy_g[side, 0, out, :] = jnp.where(
                    group == 0, parts[0],
                    jnp.where(group == 1, parts[1], jnp.where(group == 2, parts[2], parts[3])),
                )
                sy_g[side, 1, out, :] = parts[4]
        for side, row, names in ((0, EDGE, DOWN_X), (1, EDGE + ROWS - 1, UP_X)):
            for at, q in enumerate(names):
                for j in OWN:
                    sx_g[side, at, pl.ds(j - 1, 1), :] = g[q, j, pl.ds(row, 1), :]
        start(ex_g(par))

    def take_populations(par):
        finish(ex_g(par))
        for side, tile, names in ((0, 0, UP_Y), (1, NT - 1, DOWN_Y)):
            home = 3 if side == 0 else 0
            for k in range(10):
                rows = pl.ds(EDGE - 8 + 8 * k, 8)
                v = strip_rows(ry_g, par, side, 0, k)
                for at, q in enumerate(names):
                    if at == 4:
                        v = strip_rows(ry_g, par, side, 1, k)
                    g[q, tile, rows, :] = rolled(v, (home - at % 4) * BS)
        for side, row, names in ((0, EDGE - 1, UP_X), (1, EDGE + ROWS, DOWN_X)):
            for at, q in enumerate(names):
                for j in OWN:
                    g[q, j, pl.ds(row, 1), :] = rx_g[par, side, at, pl.ds(j - 1, 1), :]

    def propagate(step, tiles):
        r = own_rows(step)
        own = pl.ds(pl.multiple_of(8 * step, 8), 8)
        stream(g, f, r, own, tiles, lambda pop, j: store_moments(pop, j, r))

    def collide():
        @pl.loop(0, 8, unroll=UNROLL_LBM)
        def _(step):
            r = own_rows(step)
            own = pl.ds(pl.multiple_of(8 * step, 8), 8)
            rows = pl.ds(r, 8)
            for j in OWN:
                k = j - 1
                c0[j, rows, :] = n0[k, own, :]
                c1[j, rows, :] = n1[k, own, :]
                r0[j, rows, :] = r_next[k, own, :]
                fluid = fl[k, own, :] > 0.0
                density = rho[k, own, :]
                a = vx[k, own, :]
                b = vy[k, own, :]
                d = uz[k, own, :]
                square = a * a + b * b + d * d
                rest = 1.25 - 1.875 * square
                big = density * (1.0 / 18.0)
                small = density * (1.0 / 36.0)
                lanes = slice(k * LANES, j * LANES)
                pop0 = f[0, own, lanes]
                relaxed = density * (1.0 / 3.0) * rest - 0.25 * pop0
                g[0, j, rows, :] = jnp.where(fluid, relaxed, pop0)
                for q in range(1, Q, 2):
                    cx, cy, cz = VELOCITY[q]
                    s = None
                    for comp, val in ((cx, a), (cy, b), (cz, d)):
                        if comp:
                            if s is None:
                                s = val
                            else:
                                s = s + val if comp > 0 else s - val
                    weight = big if q < 7 else small
                    even = weight * (rest + 5.625 * (s * s))
                    odd = weight * (3.75 * s)
                    fa = f[q, own, lanes]
                    fb = f[q + 1, own, lanes]
                    g[q, j, rows, :] = jnp.where(fluid, (even + odd) - 0.25 * fa, fb)
                    g[q + 1, j, rows, :] = jnp.where(fluid, (even - odd) - 0.25 * fb, fa)

    for copy in first:
        copy.wait()

    @pl.loop(0, 8)
    def _(step):
        r = own_rows(step)
        own = pl.ds(pl.multiple_of(8 * step, 8), 8)
        for j in OWN:
            fluid = mk[j - 1, own, :] == 0
            fl[j - 1, own, :] = jnp.where(fluid, 1.0, 0.0)
            t[j, pl.ds(r, 8), :] = jnp.where(fluid, t[j, pl.ds(r, 8), :], -1.0)

    starts = (t, phi, c0, c1)
    depths = (3, 3, 2, 2)
    for j in OWN:
        at = 0
        for ref, deep in zip(starts, depths):
            for layer in range(deep):
                to = pl.ds(j - 1, 1)
                sx_i[0, at, to, :] = ref[j, pl.ds(EDGE + layer, 1), :]
                sx_i[1, at, to, :] = ref[j, pl.ds(EDGE + ROWS - 1 - layer, 1), :]
                at += 1
    for n, ref in enumerate(starts):
        for k in range(8):
            rows = pl.ds(EDGE + 8 * k, 8)
            sy_i[0, n, pl.ds(8 * k, 8), :] = ref[1, rows, :]
            sy_i[1, n, pl.ds(8 * k, 8), :] = ref[TILES, rows, :]
    first_halo = exchange(0, staged(sy_i), ry_i, sx_i, rx_i, send_i, recv_i)
    pl.semaphore_wait(barrier, N_DEV - 1)
    start(first_halo)

    for copy in pops:
        copy.wait()

    @pl.loop(0, 8)
    def _(step):
        r = own_rows(step)
        own = pl.ds(pl.multiple_of(8 * step, 8), 8)
        for j in OWN:
            store_moments(
                [f[q, own, (j - 1) * LANES : j * LANES] for q in range(Q)], j, r
            )

    send_velocity(0)

    finish(first_halo)
    for k in range(10):
        rows = pl.ds(EDGE - 8 + 8 * k, 8)
        for n, ref in enumerate(starts):
            ref[0, rows, :] = strip_rows(ry_i, 0, 0, n, k)
            ref[NT - 1, rows, :] = strip_rows(ry_i, 0, 1, n, k)
    for j in OWN:
        at = 0
        for ref, deep in zip(starts, depths):
            for layer in range(deep):
                of = pl.ds(j - 1, 1)
                ref[j, pl.ds(EDGE - 1 - layer, 1), :] = rx_i[0, 0, at, of, :]
                ref[j, pl.ds(EDGE + ROWS + layer, 1), :] = rx_i[0, 1, at, of, :]
                at += 1

    @pl.loop(0, 10)
    def _(step):
        r = pl.multiple_of(EDGE - 8 + 8 * step, 8)
        rows = pl.ds(r, 8)
        raw = {j: t[j, rows, :] for j in ALL}
        v = {j: jnp.maximum(raw[j], 0.0) for j in ALL}
        up = {}
        down = {}
        for j in ALL:
            fluid = jnp.where(raw[j] >= 0.0, 1.0, 0.0)
            xn = v[j] * jnp.maximum(t[j, pl.ds(r + 1, 8), :], 0.0)
            xp = v[j] * jnp.maximum(t[j, pl.ds(r - 1, 8), :], 0.0)
            yn = v[j] * y_next(v.get, j, up)
            yp = v[j] * y_prev(v.get, j, down)
            zn = jnp.where(z_last, 0.0, v[j] * rolled(v[j], -1))
            zp = jnp.where(z_first, 0.0, v[j] * rolled(v[j], 1))
            kx[j, rows, :] = xn
            ky[j, rows, :] = yn
            kym[j, rows, :] = yp
            kz[j, rows, :] = zn
            kzm[j, rows, :] = zp
            diagonal = SCREENING * fluid + (1.0 - fluid)
            dg[j, rows, :] = diagonal + xn + xp + yn + yp + zn + zp

    @pl.loop(0, 10)
    def _(step):
        r = pl.multiple_of(EDGE - 8 + 8 * step, 8)
        rows = pl.ds(r, 8)

        def sink(j, here_v, out):
            charge = c0[j, rows, :] - c1[j, rows, :]
            r0[j, rows, :] = jnp.where(t[j, rows, :] >= 0.0, charge, 0.0) - out

        apply(phi, r, ALL, sink)

    def body(n, tau):
        par = lax.rem(n, 2)
        nxt = 1 - par
        @pl.when(n > 0)
        def _():
            take_residual(par)


        def to_w(r, tiles):
            def sink(j, here_v, out):
                w[j, pl.ds(r, 8), :] = out - tau * here_v

            apply(r0, r, tiles, sink)

        @pl.loop(0, 8, unroll=UNROLL_APPLY)
        def _(step):
            to_w(own_rows(step), ALL)

        to_w(EDGE - 8, OWN)
        to_w(EDGE + ROWS, OWN)

        zero = jnp.zeros((8, LANES), jnp.float32)

        def sums(step, acc):
            r = own_rows(step)
            own = pl.ds(pl.multiple_of(8 * step, 8), 8)
            acc = list(acc)

            def sink(j, here_v, out):
                aw[j - 1, own, :] = out
                res = r0[j, pl.ds(r, 8), :]
                acc[0] = acc[0] + res * res
                acc[1] = acc[1] + res * here_v
                acc[2] = acc[2] + here_v * here_v
                acc[3] = acc[3] + here_v * out

            apply(w, r, OWN, sink)
            return tuple(acc)

        acc = lax.fori_loop(0, 8, sums, (zero,) * 4, unroll=UNROLL_APPLY)
        rows4 = []
        for a in acc:
            a = jnp.sum(a, axis=0, keepdims=True)
            a = jnp.broadcast_to(a, (8, LANES))
            a = a + rolled(a, 2 * BS)
            rows4.append(a + rolled(a, BS))
        mine = jnp.where(
            group == 0, rows4[0],
            jnp.where(group == 1, rows4[1], jnp.where(group == 2, rows4[2], rows4[3])),
        )[0:1]
        ar[par, me] = mine
        x4, y4 = gx // 4, lax.rem(gx, 4)
        z4, core = gy // 2, lax.rem(gy, 2)
        for a, b, d, e in tile_offsets():
            dev = (
                lax.rem(x4 + a, 4) * 4 + lax.rem(y4 + b, 4),
                lax.rem(z4 + d, 4) * 2 + lax.rem(core + e, 2),
            )
            pltpu.make_async_remote_copy(
                src_ref=ar.at[par, me], dst_ref=ar.at[par, me],
                send_sem=ar_send, recv_sem=ar_recv.at[par],
                device_id=dev, device_id_type=MESH,
            ).start()

        @pl.when(n > 0)
        def _():
            take_populations(nxt)
            border(propagate)
            send_velocity(par)
            inside(propagate)

        others = ar.at[par, pl.ds(0, N_DEV - 1)]
        pltpu.make_async_copy(others, others, ar_send).wait()
        pltpu.make_async_copy(others, others, ar_recv.at[par]).wait()
        parts = [ar[par, k] for k in range(8)]
        for k in range(8, N_DEV):
            parts[k % 8] = parts[k % 8] + ar[par, k]
        while len(parts) > 1:
            parts = [parts[k] + parts[k + 1] for k in range(0, len(parts), 2)]
        total = parts[0]
        where = lax.broadcasted_iota(jnp.int32, (1, LANES), 1) // BS
        s = [
            jnp.sum(jnp.where(where == k, total, 0.0), axis=1, keepdims=True) for k in range(4)
        ]
        ratio = s[1] / s[0]
        lam = tau + ratio
        first_len = 1.0 / lam
        square = first_len * first_len
        rr1 = square * (s[2] - ratio * ratio * s[0])
        beta = rr1 / s[0]
        curve = square * (
            ratio * ratio * lam * s[0] - 2.0 * ratio * (s[2] + tau * s[1]) + s[3]
        ) - beta * beta * lam * s[0]
        second_len = jnp.where(curve > 0.0, rr1 / jnp.where(curve > 0.0, curve, 1.0), 0.0)
        along_r = first_len + second_len * (first_len * ratio + beta)
        along_w = second_len * first_len
        cr = jnp.broadcast_to(along_r, (8, LANES))
        cw = jnp.broadcast_to(along_w, (8, LANES))
        keep_r = jnp.broadcast_to(1.0 - along_r * tau[0:1, 0:1], (8, LANES))

        def new_phi(r, tiles):
            rows = pl.ds(r, 8)
            new = [
                phi[j, rows, :] + (cr * r0[j, rows, :] - cw * w[j, rows, :]) for j in tiles
            ]
            for j, v in zip(tiles, new):
                phi[j, rows, :] = v

        @pl.loop(0, 8, unroll=UNROLL_APPLY)
        def _(step):
            new_phi(own_rows(step), ALL)

        new_phi(EDGE - 8, OWN)
        new_phi(EDGE + ROWS, OWN)
        take_velocity(par)

        def faces(k, ca, cb, da, db, pa, pb, ua, ub, half_field):
            hu = 0.25 * (ua + ub)
            hd = 0.5 * (pb - pa)
            if half_field:
                hd = hd - half_field
            return (
                k * ((ca - cb) + (ca + cb) * (hu - hd)),
                k * ((da - db) + (da + db) * (hu + hd)),
            )

        def x_faces(j, r):
            rows = pl.ds(r, 8)
            more = pl.ds(r + 1, 8)
            out = faces(
                kx[j, rows, :],
                c0[j, rows, :], c0[j, more, :], c1[j, rows, :], c1[j, more, :],
                phi[j, rows, :], phi[j, more, :], ux[j, rows, :], ux[j, more, :], 0.5 * APPLIED,
            )
            flux0[j - 1, rows, :] = out[0]
            flux1[j - 1, rows, :] = out[1]

        @pl.loop(0, 9, unroll=UNROLL_XFLUX)
        def _(step):
            for j in OWN:
                x_faces(j, pl.multiple_of(EDGE - 8 + 8 * step, 8))

        def y_faces(step, tiles):
            r = own_rows(step)
            rows = pl.ds(r, 8)
            own = pl.ds(pl.multiple_of(8 * step, 8), 8)
            p, a, b, v = [loader(ref, rows) for ref in (phi, c0, c1, uy)]
            caches = [{} for _ in range(8)]
            for j in tiles:
                pn, an, bn, vn = [y_next(ld, j, ca) for ld, ca in zip((p, a, b, v), caches)]
                pp, ap, bp, vp = [y_prev(ld, j, ca) for ld, ca in zip((p, a, b, v), caches[4:])]
                pj, aj, bj, vj = p(j), a(j), b(j), v(j)
                f0, f1 = faces(ky[j, rows, :], aj, an, bj, bn, pj, pn, vj, vn, 0.0)
                g0, g1 = faces(kym[j, rows, :], ap, aj, bp, bj, pp, pj, vp, vj, 0.0)
                dy0[j - 1, own, :] = f0 - g0
                dy1[j - 1, own, :] = f1 - g1
                slope[j - 1, own, :] = pn - pp

        def z_faces(step, tiles):
            rows = pl.ds(own_rows(step), 8)
            own = pl.ds(pl.multiple_of(8 * step, 8), 8)
            for j in tiles:
                here_v = (c0[j, rows, :], c1[j, rows, :], phi[j, rows, :], uz[j - 1, own, :])
                aj, bj, pj, vj = here_v
                an, bn, pn, vn = [rolled(v, -1) for v in here_v]
                ap, bp, pp, vp = [rolled(v, 1) for v in here_v]
                f0, f1 = faces(kz[j, rows, :], aj, an, bj, bn, pj, pn, vj, vn, 0.0)
                g0, g1 = faces(kzm[j, rows, :], ap, aj, bp, bj, pp, pj, vp, vj, 0.0)
                dz0[j - 1, own, :] = f0 - g0
                dz1[j - 1, own, :] = f1 - g1

        def transport_step(step, tiles):
            r = own_rows(step)
            rows = pl.ds(r, 8)
            less = pl.ds(r - 1, 8)
            own = pl.ds(pl.multiple_of(8 * step, 8), 8)
            for j in tiles:
                k = j - 1
                d0 = flux0[k, rows, :] - flux0[k, less, :] + dy0[k, own, :] + dz0[k, own, :]
                d1 = flux1[k, rows, :] - flux1[k, less, :] + dy1[k, own, :] + dz1[k, own, :]
                aj = c0[j, rows, :]
                bj = c1[j, rows, :]
                new0 = aj - ION_STEP * d0
                new1 = bj - ION_STEP * d1
                n0[k, own, :] = new0
                n1[k, own, :] = new1
                charge = new0 - new1
                push = (FORCE_SCALE * RELAX_TIME) * charge * rinv[k, own, :]
                vx[k, own, :] = ux[j, rows, :] + push * (
                    APPLIED - 0.5 * (phi[j, pl.ds(r + 1, 8), :] - phi[j, less, :])
                )
                vy[k, own, :] = uy[j, rows, :] - push * (0.5 * slope[k, own, :])
                r_next[k, own, :] = (
                    keep_r * r0[j, rows, :] - cr * w[j, rows, :] + cw * aw[k, own, :]
                    + fl[k, own, :] * (charge - (aj - bj))
                )

        border(y_faces)
        border(z_faces)
        border(transport_step)

        @pl.when(n < STEPS - 1)
        def _():
            send_residual(nxt)

        inside(y_faces)
        inside(z_faces)
        inside(transport_step)
        collide()
        send_populations(par)
        return jnp.broadcast_to(lam, (8, LANES))

    lax.fori_loop(0, STEPS, body, jnp.ones((8, LANES), jnp.float32))

    own = pl.ds(EDGE, ROWS)
    out = [(g.at[:, pl.ds(1, TILES), own, :], g_out.at[:, pl.ds(1, TILES), own, :])]
    for j in range(TILES):
        lanes = pl.ds(j * LANES, LANES)
        out.append((phi.at[1 + j, own, :], pot_out.at[:, lanes]))
        out.append((c0.at[1 + j, own, :], conc_out.at[0, :, lanes]))
        out.append((c1.at[1 + j, own, :], conc_out.at[1, :, lanes]))
    done = [pltpu.make_async_copy(s, d, out_sem.at[n]) for n, (s, d) in enumerate(out)]
    start(done)
    take_populations((STEPS - 1) % 2)
    rims = [
        pltpu.make_async_copy(g.at[part], g_out.at[part], out_sem.at[len(done) + n])
        for n, part in enumerate(ghost_parts())
    ]
    start(rims)
    finish(done + rims)


def ghost_parts():
    parts = [(q, pl.ds(0, 1), pl.ds(EDGE - 8, ROWS + 16)) for q in UP_Y]
    parts += [(q, pl.ds(NT - 1, 1), pl.ds(EDGE - 8, ROWS + 16)) for q in DOWN_Y]
    parts += [(q, pl.ds(1, TILES), pl.ds(EDGE - 8, 8)) for q in UP_X]
    parts += [(q, pl.ds(1, TILES), pl.ds(EDGE + ROWS, 8)) for q in DOWN_X]
    return parts


def last_kernel(
    g_hbm, conc_hbm, pot_hbm, pop_out, conc_out, pot_out, g, f, conc, pot, in_sem, out_sem
):
    rims = [
        pltpu.make_async_copy(g_hbm.at[part], g.at[part], in_sem.at[4 + n])
        for n, part in enumerate(ghost_parts())
    ]
    chunks = []
    for n, (low, high) in enumerate(((16, 40), (40, 56), (56, 72), (72, 80))):
        part = (slice(None), pl.ds(1, TILES), pl.ds(low, high - low))
        chunks.append(pltpu.make_async_copy(g_hbm.at[part], g.at[part], in_sem.at[n]))
    chunks[0].start()
    for copy in rims:
        copy.start()
    for copy in chunks[1:]:
        copy.start()
    small = [
        pltpu.make_async_copy(conc_hbm, conc, in_sem.at[24]),
        pltpu.make_async_copy(pot_hbm, pot, in_sem.at[25]),
    ]
    for copy in small:
        copy.start()
    others = [
        pltpu.make_async_copy(conc, conc_out, out_sem.at[4]),
        pltpu.make_async_copy(pot, pot_out, out_sem.at[5]),
    ]
    for copy in rims:
        copy.wait()
    outs = []
    for n in range(4):
        chunks[n].wait()
        for step in (2 * n, 2 * n + 1):
            stream(g, f, EDGE + 8 * step, pl.ds(8 * step, 8), range(1, TILES + 1), None)
        part = (slice(None), pl.ds(16 * n, 16))
        outs.append(pltpu.make_async_copy(f.at[part], pop_out.at[part], out_sem.at[n]))
        outs[-1].start()
        if n == 0:
            for copy in small:
                copy.wait()
            for copy in others:
                copy.start()
    for copy in outs + others:
        copy.wait()


def local(populations, concentration, potential, mobility, solid_mask, block_col):
    anywhere = pl.BlockSpec(memory_space=pl.ANY)
    f32 = jnp.float32

    def field(*lead):
        return pltpu.VMEM(lead + (NT, NR, LANES), f32)

    def bare(*lead):
        return pltpu.VMEM(lead + (TILES, ROWS, LANES), f32)

    def vm(*shape):
        return pltpu.VMEM(shape + (LANES,), f32)

    scratch = [
        pltpu.VMEM((Q, ROWS, TILES * LANES), f32), field(Q),
        field(), field(), field(), bare(), field(), field(), bare(), bare(), field(),
        field(), field(), field(), field(), field(), field(), bare(),
        pltpu.VMEM((TILES, ROWS, LANES), jnp.int32),
        field(), field(), bare(), bare(), bare(), bare(), bare(),
        vm(TILES, NR), vm(TILES, NR), bare(), bare(), bare(), bare(), bare(), bare(),
        vm(2, N_DEV, 1),
        vm(2, 1, ROWS), vm(2, 2, 1, STRIP), vm(2, 4, 8), vm(2, 2, 4, 8),
        vm(2, 2, ROWS), vm(2, 2, 2, STRIP), vm(2, 5, 8), vm(2, 2, 5, 8),
        vm(2, 1, 8), vm(2, 2, 1, STRIP), vm(2, 2, 1, 8),
        vm(2, 4, ROWS), vm(1, 2, 4, STRIP), vm(2, 10, 8), vm(1, 2, 10, 8),
        pltpu.SemaphoreType.DMA((48,)),
        pltpu.SemaphoreType.DMA((48,)),
        pltpu.SemaphoreType.DMA,
        pltpu.SemaphoreType.DMA((2,)),
        pltpu.SemaphoreType.DMA((8,)), pltpu.SemaphoreType.DMA((2, 8)),
        pltpu.SemaphoreType.DMA((8,)), pltpu.SemaphoreType.DMA((2, 8)),
        pltpu.SemaphoreType.DMA((8,)), pltpu.SemaphoreType.DMA((2, 8)),
        pltpu.SemaphoreType.DMA((8,)), pltpu.SemaphoreType.DMA((1, 8)),
    ]
    flat = (ROWS, TILES * LANES)
    g_last, conc, pot = pl.pallas_call(
        kernel,
        out_shape=(
            jax.ShapeDtypeStruct((Q, NT, NR, LANES), f32),
            jax.ShapeDtypeStruct((2,) + flat, f32),
            jax.ShapeDtypeStruct(flat, f32),
        ),
        in_specs=[pl.BlockSpec(memory_space=pltpu.SMEM)] + [anywhere] * 5,
        out_specs=(anywhere,) * 3,
        scratch_shapes=scratch,
        compiler_params=pltpu.CompilerParams(
            collective_id=0, has_side_effects=True, vmem_limit_bytes=VMEM_LIMIT
        ),
        cost_estimate=pl.CostEstimate(
            flops=100_000_000, bytes_accessed=12_000_000, transcendentals=0
        ),
    )(
        block_col,
        populations.reshape((Q,) + flat),
        concentration.reshape((2,) + flat),
        potential.reshape(flat),
        mobility.reshape(flat),
        solid_mask.reshape(flat),
    )
    pop, conc, pot = pl.pallas_call(
        last_kernel,
        out_shape=(
            jax.ShapeDtypeStruct((Q,) + flat, f32),
            jax.ShapeDtypeStruct((2,) + flat, f32),
            jax.ShapeDtypeStruct(flat, f32),
        ),
        in_specs=[anywhere] * 3,
        out_specs=(anywhere,) * 3,
        scratch_shapes=[
            pltpu.VMEM((Q, NT, NR, LANES), f32),
            pltpu.VMEM((Q,) + flat, f32),
            pltpu.VMEM((2,) + flat, f32),
            pltpu.VMEM(flat, f32),
            pltpu.SemaphoreType.DMA((26,)),
            pltpu.SemaphoreType.DMA((6,)),
        ],
        compiler_params=pltpu.CompilerParams(vmem_limit_bytes=VMEM_LIMIT),
        cost_estimate=pl.CostEstimate(
            flops=10_000_000, bytes_accessed=12_000_000, transcendentals=0
        ),
    )(g_last, conc, pot)
    return (
        pop.reshape(populations.shape),
        conc.reshape(concentration.shape),
        pot.reshape(potential.shape),
    )


def solution(mesh):
    split = ("gx", "gy")
    return jax.shard_map(
        local,
        mesh=mesh,
        in_specs=(
            P(None, split, None, None),
            P(None, split, None, None),
            P(split, None, None),
            P(split, None, None),
            P(split, None, None),
            P(),
        ),
        out_specs=(P(None, split, None, None), P(None, split, None, None), P(split, None, None)),
        check_vma=False,
    )
```

time: 120 us -> 99.5 us (0.83)
  local copies, waits for them, and re-layouts: 11.5 us -> 0 us
  Pallas kernels: 107 us -> 98.8 us
    unnamed x13 -> x0, local copies, waits for them, and re-layouts: 11.5 us -> none
    pallas_call x1 -> x2, Pallas kernels: 107 us -> 98.8 us  [the longest x1 93.3 us: local(): pl.pallas_call(kernel, out_shape=(jax.ShapeDtypeStruct((Q, NT, NR, LANES)...]
where the time goes in v2:
time: 99.5 us; the launch traced here: 99.4 us
  Pallas kernels  98.8 us (99%)
    pallas_call x1, Pallas kernels, local(): pl.pallas_call(kernel, out_shape=(jax.ShapeDtypeStruct((Q, NT, NR, LANES)...  93.3 us
    pallas_call x1, Pallas kernels, local(): pl.pallas_call(last_kernel, out_shape=(jax.ShapeDtypeStruct((Q,) + flat,...  5.48 us

profile of v2, /device:TPU:0, one launch (start us, length us, event | category | flops | bytes accessed | tf_op | source)
XLA Modules:
  0.0 99.4 jit_solution(10187073965914709923)
XLA Ops:
  0.6 93.3 %shard_map.85 = (f32[19,10,96,128]{3,2,1,0:T(8,128)}, f32[2,64,1024]{2,1,0:T(8,128)}, f32[64,1024]{1,0:T(8,128)}) custom-call(s32[256]{0:T(256)} %col_ref.1, f32[19,64,1024]{2,1,0:T(8,128)} %bitcast.8, f32[2,64,1024]{2,1,0:T(8,128)} %bitcast.9, f32[64,1024]{1,0:T(8,128)} %bitcast.10, f32[64,1024]{1,0:T(8,128)} %bitcast.11, s32[64,1024]{1,0:T(8,128)} %bitcast.12), custom_call_target="tpu_custom_call" | custom-call | flops 100000000 | bytes 12000000 | tf_op jit(solution)/shard_map/pallas_call | solution.py:865
  93.9 5.5 %shard_map.86 = (f32[19,64,1024]{2,1,0:T(8,128)}, f32[2,64,1024]{2,1,0:T(8,128)}, f32[64,1024]{1,0:T(8,128)}) custom-call(f32[19,10,96,128]{3,2,1,0:T(8,128)} %get-tuple-element.9.g_hbm, f32[2,64,1024]{2,1,0:T(8,128)} %get-tuple-element.10.conc_hbm, f32[64,1024]{1,0:T(8,128)} %get-tuple-element.11.pot_hbm), custom_call_target="tpu_custom_call" | custom-call | flops 10000000 | bytes 12000000 | tf_op jit(solution)/shard_map/pallas_call | solution.py:889

commit v3 on v2

--- a/solution.py
+++ b/solution.py
@@ -52,8 +52,7 @@
 NT = TILES + 2
 VMEM_LIMIT = 60 * 1024 * 1024
 UNROLL_APPLY = 4
-UNROLL_XFLUX = 1
-UNROLL_BORDER = 2
+UNROLL_BORDER = 3
 UNROLL_INSIDE = 2
 UNROLL_LBM = 2
 SIDE = 40
@@ -110,7 +109,7 @@
     col_ref, pop_hbm, conc_hbm, pot_hbm, mob_hbm, mask_hbm,
     g_out, conc_out, pot_out,
     f, g, phi, r0, w, aw, c0, c1, n0, n1, t, kx, ky, kym, kz, kzm, dg, fl, mk,
-    ux, uy, uz, rho, rinv, vx, vy, flux0, flux1, dy0, dy1, dz0, dz1, slope, r_next,
+    ux, uy, uz, rho, rinv, vx, vy, dy0, dy1, dz0, dz1, slope, r_next,
     ar, sy_r, ry_r, sx_r, rx_r, sy_g, ry_g, sx_g, rx_g, sx_u, ry_u, rx_u, sy_i, ry_i, sx_i, rx_i,
     in_sem, out_sem, ar_send, ar_recv, send_r, recv_r, send_g, recv_g, send_u, recv_u,
     send_i, recv_i,
@@ -128,6 +127,15 @@
     group = lane // BS
     z_first = depth == 0
     z_last = depth == BS - 1
+
+    x4, y4 = gx // 4, lax.rem(gx, 4)
+    z4, core = gy // 2, lax.rem(gy, 2)
+    to_gx = {
+        (a, b): lax.rem(x4 + a, 4) * 4 + lax.rem(y4 + b, 4) for a in range(4) for b in range(4)
+    }
+    to_gy = {
+        (d, e): lax.rem(z4 + d, 4) * 2 + lax.rem(core + e, 2) for d in range(4) for e in range(2)
+    }
 
     loads = []
     for j in range(TILES):
@@ -278,6 +286,32 @@
         def _(step):
             work(step, OWN[1:-1])
 
+    def rim(work):
+        @pl.loop(0, 2, unroll=True)
+        def _(k):
+            work(7 * k, ALL)
+
+        @pl.loop(1, 7, unroll=UNROLL_BORDER)
+        def _(step):
+            work(step, ALL[:2])
+            work(step, ALL[-2:])
+
+    def rows_beyond(work, tiles=OWN):
+        @pl.loop(0, 2, unroll=True)
+        def _(k):
+            work(9 * k - 1, tiles)
+
+    def to_w(tau):
+        def work(step, tiles):
+            r = own_rows(step)
+
+            def sink(j, here_v, out):
+                w[j, pl.ds(r, 8), :] = out - tau * here_v
+
+            apply(r0, r, tiles, sink)
+
+        return work
+
     def moments(pop):
         p = pop
         xp = p[7] + p[9] + p[11] + p[13] + p[1]
@@ -406,46 +440,41 @@
         own = pl.ds(pl.multiple_of(8 * step, 8), 8)
         stream(g, f, r, own, tiles, lambda pop, j: store_moments(pop, j, r))
 
-    def collide():
-        @pl.loop(0, 8, unroll=UNROLL_LBM)
-        def _(step):
-            r = own_rows(step)
-            own = pl.ds(pl.multiple_of(8 * step, 8), 8)
-            rows = pl.ds(r, 8)
-            for j in OWN:
-                k = j - 1
-                c0[j, rows, :] = n0[k, own, :]
-                c1[j, rows, :] = n1[k, own, :]
-                r0[j, rows, :] = r_next[k, own, :]
-                fluid = fl[k, own, :] > 0.0
-                density = rho[k, own, :]
-                a = vx[k, own, :]
-                b = vy[k, own, :]
-                d = uz[k, own, :]
-                square = a * a + b * b + d * d
-                rest = 1.25 - 1.875 * square
-                big = density * (1.0 / 18.0)
-                small = density * (1.0 / 36.0)
-                lanes = slice(k * LANES, j * LANES)
-                pop0 = f[0, own, lanes]
-                relaxed = density * (1.0 / 3.0) * rest - 0.25 * pop0
-                g[0, j, rows, :] = jnp.where(fluid, relaxed, pop0)
-                for q in range(1, Q, 2):
-                    cx, cy, cz = VELOCITY[q]
-                    s = None
-                    for comp, val in ((cx, a), (cy, b), (cz, d)):
-                        if comp:
-                            if s is None:
-                                s = val
-                            else:
-                                s = s + val if comp > 0 else s - val
-                    weight = big if q < 7 else small
-                    even = weight * (rest + 5.625 * (s * s))
-                    odd = weight * (3.75 * s)
-                    fa = f[q, own, lanes]
-                    fb = f[q + 1, own, lanes]
-                    g[q, j, rows, :] = jnp.where(fluid, (even + odd) - 0.25 * fa, fb)
-                    g[q + 1, j, rows, :] = jnp.where(fluid, (even - odd) - 0.25 * fb, fa)
+    def collide(step, tiles):
+        r = own_rows(step)
+        own = pl.ds(pl.multiple_of(8 * step, 8), 8)
+        rows = pl.ds(r, 8)
+        for j in tiles:
+            k = j - 1
+            fluid = fl[k, own, :] > 0.0
+            density = rho[k, own, :]
+            a = vx[k, own, :]
+            b = vy[k, own, :]
+            d = uz[k, own, :]
+            square = a * a + b * b + d * d
+            rest = 1.25 - 1.875 * square
+            big = density * (1.0 / 18.0)
+            small = density * (1.0 / 36.0)
+            lanes = slice(k * LANES, j * LANES)
+            pop0 = f[0, own, lanes]
+            relaxed = density * (1.0 / 3.0) * rest - 0.25 * pop0
+            g[0, j, rows, :] = jnp.where(fluid, relaxed, pop0)
+            for q in range(1, Q, 2):
+                cx, cy, cz = VELOCITY[q]
+                s = None
+                for comp, val in ((cx, a), (cy, b), (cz, d)):
+                    if comp:
+                        if s is None:
+                            s = val
+                        else:
+                            s = s + val if comp > 0 else s - val
+                weight = big if q < 7 else small
+                even = weight * (rest + 5.625 * (s * s))
+                odd = weight * (3.75 * s)
+                fa = f[q, own, lanes]
+                fb = f[q + 1, own, lanes]
+                g[q, j, rows, :] = jnp.where(fluid, (even + odd) - 0.25 * fa, fb)
+                g[q + 1, j, rows, :] = jnp.where(fluid, (even - odd) - 0.25 * fb, fa)
 
     for copy in first:
         copy.wait()
@@ -478,6 +507,44 @@
     pl.semaphore_wait(barrier, N_DEV - 1)
     start(first_halo)
 
+    def coefficients(step, tiles):
+        r = own_rows(step)
+        rows = pl.ds(r, 8)
+
+        def load(j):
+            return jnp.maximum(t[j, rows, :], 0.0)
+
+        up = {}
+        down = {}
+        for j in tiles:
+            raw = t[j, rows, :]
+            v = load(j)
+            fluid = jnp.where(raw >= 0.0, 1.0, 0.0)
+            xn = v * jnp.maximum(t[j, pl.ds(r + 1, 8), :], 0.0)
+            xp = v * jnp.maximum(t[j, pl.ds(r - 1, 8), :], 0.0)
+            yn = v * y_next(load, j, up)
+            yp = v * y_prev(load, j, down)
+            zn = jnp.where(z_last, 0.0, v * rolled(v, -1))
+            zp = jnp.where(z_first, 0.0, v * rolled(v, 1))
+            kx[j, rows, :] = xn
+            ky[j, rows, :] = yn
+            kym[j, rows, :] = yp
+            kz[j, rows, :] = zn
+            kzm[j, rows, :] = zp
+            diagonal = SCREENING * fluid + (1.0 - fluid)
+            dg[j, rows, :] = diagonal + xn + xp + yn + yp + zn + zp
+
+    def first_residual(step, tiles):
+        r = own_rows(step)
+        rows = pl.ds(r, 8)
+
+        def sink(j, here_v, out):
+            charge = c0[j, rows, :] - c1[j, rows, :]
+            r0[j, rows, :] = jnp.where(t[j, rows, :] >= 0.0, charge, 0.0) - out
+
+        apply(phi, r, tiles, sink)
+
+    inside(coefficients)
     for copy in pops:
         copy.wait()
 
@@ -507,40 +574,11 @@
                 ref[j, pl.ds(EDGE + ROWS + layer, 1), :] = rx_i[0, 1, at, of, :]
                 at += 1
 
-    @pl.loop(0, 10)
-    def _(step):
-        r = pl.multiple_of(EDGE - 8 + 8 * step, 8)
-        rows = pl.ds(r, 8)
-        raw = {j: t[j, rows, :] for j in ALL}
-        v = {j: jnp.maximum(raw[j], 0.0) for j in ALL}
-        up = {}
-        down = {}
-        for j in ALL:
-            fluid = jnp.where(raw[j] >= 0.0, 1.0, 0.0)
-            xn = v[j] * jnp.maximum(t[j, pl.ds(r + 1, 8), :], 0.0)
-            xp = v[j] * jnp.maximum(t[j, pl.ds(r - 1, 8), :], 0.0)
-            yn = v[j] * y_next(v.get, j, up)
-            yp = v[j] * y_prev(v.get, j, down)
-            zn = jnp.where(z_last, 0.0, v[j] * rolled(v[j], -1))
-            zp = jnp.where(z_first, 0.0, v[j] * rolled(v[j], 1))
-            kx[j, rows, :] = xn
-            ky[j, rows, :] = yn
-            kym[j, rows, :] = yp
-            kz[j, rows, :] = zn
-            kzm[j, rows, :] = zp
-            diagonal = SCREENING * fluid + (1.0 - fluid)
-            dg[j, rows, :] = diagonal + xn + xp + yn + yp + zn + zp
-
-    @pl.loop(0, 10)
-    def _(step):
-        r = pl.multiple_of(EDGE - 8 + 8 * step, 8)
-        rows = pl.ds(r, 8)
-
-        def sink(j, here_v, out):
-            charge = c0[j, rows, :] - c1[j, rows, :]
-            r0[j, rows, :] = jnp.where(t[j, rows, :] >= 0.0, charge, 0.0) - out
-
-        apply(phi, r, ALL, sink)
+    rim(coefficients)
+    rows_beyond(coefficients, ALL)
+    rim(first_residual)
+    rows_beyond(first_residual, ALL)
+    inside(first_residual)
 
     def body(n, tau):
         par = lax.rem(n, 2)
@@ -550,18 +588,9 @@
             take_residual(par)
 
 
-        def to_w(r, tiles):
-            def sink(j, here_v, out):
-                w[j, pl.ds(r, 8), :] = out - tau * here_v
-
-            apply(r0, r, tiles, sink)
-
-        @pl.loop(0, 8, unroll=UNROLL_APPLY)
-        def _(step):
-            to_w(own_rows(step), ALL)
-
-        to_w(EDGE - 8, OWN)
-        to_w(EDGE + ROWS, OWN)
+        make_w = to_w(tau)
+        rim(make_w)
+        rows_beyond(make_w)
 
         zero = jnp.zeros((8, LANES), jnp.float32)
 
@@ -593,13 +622,8 @@
             jnp.where(group == 1, rows4[1], jnp.where(group == 2, rows4[2], rows4[3])),
         )[0:1]
         ar[par, me] = mine
-        x4, y4 = gx // 4, lax.rem(gx, 4)
-        z4, core = gy // 2, lax.rem(gy, 2)
         for a, b, d, e in tile_offsets():
-            dev = (
-                lax.rem(x4 + a, 4) * 4 + lax.rem(y4 + b, 4),
-                lax.rem(z4 + d, 4) * 2 + lax.rem(core + e, 2),
-            )
+            dev = (to_gx[a, b], to_gy[d, e])
             pltpu.make_async_remote_copy(
                 src_ref=ar.at[par, me], dst_ref=ar.at[par, me],
                 send_sem=ar_send, recv_sem=ar_recv.at[par],
@@ -627,14 +651,15 @@
             jnp.sum(jnp.where(where == k, total, 0.0), axis=1, keepdims=True) for k in range(4)
         ]
         ratio = s[1] / s[0]
-        lam = tau + ratio
+        lam = tau[0:1, 0:1] + ratio
         first_len = 1.0 / lam
         square = first_len * first_len
         rr1 = square * (s[2] - ratio * ratio * s[0])
         beta = rr1 / s[0]
         curve = square * (
-            ratio * ratio * lam * s[0] - 2.0 * ratio * (s[2] + tau * s[1]) + s[3]
+            ratio * ratio * lam * s[0] - 2.0 * ratio * (s[2] + tau[0:1, 0:1] * s[1]) + s[3]
         ) - beta * beta * lam * s[0]
+        lam_all = jnp.broadcast_to(lam, (8, LANES))
         second_len = jnp.where(curve > 0.0, rr1 / jnp.where(curve > 0.0, curve, 1.0), 0.0)
         along_r = first_len + second_len * (first_len * ratio + beta)
         along_w = second_len * first_len
@@ -667,22 +692,6 @@
                 k * ((ca - cb) + (ca + cb) * (hu - hd)),
                 k * ((da - db) + (da + db) * (hu + hd)),
             )
-
-        def x_faces(j, r):
-            rows = pl.ds(r, 8)
-            more = pl.ds(r + 1, 8)
-            out = faces(
-                kx[j, rows, :],
-                c0[j, rows, :], c0[j, more, :], c1[j, rows, :], c1[j, more, :],
-                phi[j, rows, :], phi[j, more, :], ux[j, rows, :], ux[j, more, :], 0.5 * APPLIED,
-            )
-            flux0[j - 1, rows, :] = out[0]
-            flux1[j - 1, rows, :] = out[1]
-
-        @pl.loop(0, 9, unroll=UNROLL_XFLUX)
-        def _(step):
-            for j in OWN:
-                x_faces(j, pl.multiple_of(EDGE - 8 + 8 * step, 8))
 
         def y_faces(step, tiles):
             r = own_rows(step)
@@ -717,22 +726,25 @@
             r = own_rows(step)
             rows = pl.ds(r, 8)
             less = pl.ds(r - 1, 8)
+            more = pl.ds(r + 1, 8)
             own = pl.ds(pl.multiple_of(8 * step, 8), 8)
             for j in tiles:
                 k = j - 1
-                d0 = flux0[k, rows, :] - flux0[k, less, :] + dy0[k, own, :] + dz0[k, own, :]
-                d1 = flux1[k, rows, :] - flux1[k, less, :] + dy1[k, own, :] + dz1[k, own, :]
-                aj = c0[j, rows, :]
-                bj = c1[j, rows, :]
+                aj, bj, pj, vj = [ref[j, rows, :] for ref in (c0, c1, phi, ux)]
+                an, bn, pn, vn = [ref[j, more, :] for ref in (c0, c1, phi, ux)]
+                ap, bp, pp, vp = [ref[j, less, :] for ref in (c0, c1, phi, ux)]
+                half = 0.5 * APPLIED
+                f0, f1 = faces(kx[j, rows, :], aj, an, bj, bn, pj, pn, vj, vn, half)
+                g0, g1 = faces(kx[j, less, :], ap, aj, bp, bj, pp, pj, vp, vj, half)
+                d0 = f0 - g0 + dy0[k, own, :] + dz0[k, own, :]
+                d1 = f1 - g1 + dy1[k, own, :] + dz1[k, own, :]
                 new0 = aj - ION_STEP * d0
                 new1 = bj - ION_STEP * d1
                 n0[k, own, :] = new0
                 n1[k, own, :] = new1
                 charge = new0 - new1
                 push = (FORCE_SCALE * RELAX_TIME) * charge * rinv[k, own, :]
-                vx[k, own, :] = ux[j, rows, :] + push * (
-                    APPLIED - 0.5 * (phi[j, pl.ds(r + 1, 8), :] - phi[j, less, :])
-                )
+                vx[k, own, :] = vj + push * (APPLIED - 0.5 * (pn - pp))
                 vy[k, own, :] = uy[j, rows, :] - push * (0.5 * slope[k, own, :])
                 r_next[k, own, :] = (
                     keep_r * r0[j, rows, :] - cr * w[j, rows, :] + cw * aw[k, own, :]
@@ -747,14 +759,28 @@
         def _():
             send_residual(nxt)
 
+        border(collide)
+        send_populations(par)
         inside(y_faces)
         inside(z_faces)
         inside(transport_step)
-        collide()
-        send_populations(par)
-        return jnp.broadcast_to(lam, (8, LANES))
-
-    lax.fori_loop(0, STEPS, body, jnp.ones((8, LANES), jnp.float32))
+        inside(collide)
+
+        @pl.loop(0, 8, unroll=2)
+        def _(step):
+            rows = pl.ds(own_rows(step), 8)
+            own = pl.ds(pl.multiple_of(8 * step, 8), 8)
+            for j in OWN:
+                c0[j, rows, :] = n0[j - 1, own, :]
+                c1[j, rows, :] = n1[j - 1, own, :]
+                r0[j, rows, :] = r_next[j - 1, own, :]
+
+        inside(to_w(lam_all))
+        return lam_all
+
+    one = jnp.ones((8, LANES), jnp.float32)
+    inside(to_w(one))
+    lax.fori_loop(0, STEPS, body, one)
 
     own = pl.ds(EDGE, ROWS)
     out = [(g.at[:, pl.ds(1, TILES), own, :], g_out.at[:, pl.ds(1, TILES), own, :])]
@@ -846,7 +872,7 @@
         field(), field(), field(), field(), field(), field(), bare(),
         pltpu.VMEM((TILES, ROWS, LANES), jnp.int32),
         field(), field(), bare(), bare(), bare(), bare(), bare(),
-        vm(TILES, NR), vm(TILES, NR), bare(), bare(), bare(), bare(), bare(), bare(),
+        bare(), bare(), bare(), bare(), bare(), bare(),
         vm(2, N_DEV, 1),
         vm(2, 1, ROWS), vm(2, 2, 1, STRIP), vm(2, 4, 8), vm(2, 2, 4, 8),
         vm(2, 2, ROWS), vm(2, 2, 2, STRIP), vm(2, 5, 8), vm(2, 2, 5, 8),

time: 99.5 us -> 90.8 us (0.913)
  Pallas kernels: 98.8 us -> 90 us
    pallas_call x1, Pallas kernels: 93.3 us -> 84.5 us  [local(): pl.pallas_call(kernel, out_shape=(jax.ShapeDtypeStruct((Q, NT, NR, LANES)...]
where the time goes in v3:
time: 90.8 us; the launch traced here: 90.7 us
  Pallas kernels  90 us (99%)
    pallas_call x1, Pallas kernels, local(): pl.pallas_call(kernel, out_shape=(jax.ShapeDtypeStruct((Q, NT, NR, LANES)...  84.5 us
    pallas_call x1, Pallas kernels, local(): pl.pallas_call(last_kernel, out_shape=(jax.ShapeDtypeStruct((Q,) + flat,...  5.48 us

profile of v3, /device:TPU:0, one launch (start us, length us, event | category | flops | bytes accessed | tf_op | source)
XLA Modules:
  0.0 90.7 jit_solution(2133254017757265584)
XLA Ops:
  0.6 84.5 %shard_map.85 = (f32[19,10,96,128]{3,2,1,0:T(8,128)}, f32[2,64,1024]{2,1,0:T(8,128)}, f32[64,1024]{1,0:T(8,128)}) custom-call(s32[256]{0:T(256)} %col_ref.1, f32[19,64,1024]{2,1,0:T(8,128)} %bitcast.8, f32[2,64,1024]{2,1,0:T(8,128)} %bitcast.9, f32[64,1024]{1,0:T(8,128)} %bitcast.10, f32[64,1024]{1,0:T(8,128)} %bitcast.11, s32[64,1024]{1,0:T(8,128)} %bitcast.12), custom_call_target="tpu_custom_call" | custom-call | flops 100000000 | bytes 12000000 | tf_op jit(solution)/shard_map/pallas_call | solution.py:891
  85.2 5.5 %shard_map.86 = (f32[19,64,1024]{2,1,0:T(8,128)}, f32[2,64,1024]{2,1,0:T(8,128)}, f32[64,1024]{1,0:T(8,128)}) custom-call(f32[19,10,96,128]{3,2,1,0:T(8,128)} %get-tuple-element.9.g_hbm, f32[2,64,1024]{2,1,0:T(8,128)} %get-tuple-element.10.conc_hbm, f32[64,1024]{1,0:T(8,128)} %get-tuple-element.11.pot_hbm), custom_call_target="tpu_custom_call" | custom-call | flops 10000000 | bytes 12000000 | tf_op jit(solution)/shard_map/pallas_call | solution.py:915

commit v4 on v3

--- a/solution.py
+++ b/solution.py
@@ -137,6 +137,12 @@
         (d, e): lax.rem(z4 + d, 4) * 2 + lax.rem(core + e, 2) for d in range(4) for e in range(2)
     }
 
+    barrier = pltpu.get_barrier_semaphore()
+    for a, b, d, e in tile_offsets():
+        pl.semaphore_signal(
+            barrier, inc=1, device_id=(to_gx[a, b], to_gy[d, e]), device_id_type=MESH
+        )
+
     loads = []
     for j in range(TILES):
         lanes = pl.ds(j * LANES, LANES)
@@ -152,17 +158,6 @@
         copy.start()
     for copy in pops:
         copy.start()
-
-    barrier = pltpu.get_barrier_semaphore()
-
-    def greet(k, _):
-        other = lax.rem(me + k, N_DEV)
-        pl.semaphore_signal(
-            barrier, inc=1, device_id=(other // N_GY, lax.rem(other, N_GY)), device_id_type=MESH
-        )
-        return 0
-
-    lax.fori_loop(1, N_DEV, greet, 0)
 
     def exchange(par, strip_src, strip_dst, x_src, x_dst, send, recv):
         copies = []

time: 90.8 us -> 89 us (0.980)
  Pallas kernels: 90 us -> 88.3 us
    pallas_call x1, Pallas kernels: 84.5 us -> 82.8 us  [local(): pl.pallas_call(kernel, out_shape=(jax.ShapeDtypeStruct((Q, NT, NR, LANES)...]
where the time goes in v4:
time: 89 us; the launch traced here: 88.9 us
  Pallas kernels  88.3 us (99%)
    pallas_call x1, Pallas kernels, local(): pl.pallas_call(kernel, out_shape=(jax.ShapeDtypeStruct((Q, NT, NR, LANES)...  82.8 us
    pallas_call x1, Pallas kernels, local(): pl.pallas_call(last_kernel, out_shape=(jax.ShapeDtypeStruct((Q,) + flat,...  5.48 us

profile of v4, /device:TPU:0, one launch (start us, length us, event | category | flops | bytes accessed | tf_op | source)
XLA Modules:
  0.0 88.9 jit_solution(16135863755482637833)
XLA Ops:
  0.6 82.8 %shard_map.85 = (f32[19,10,96,128]{3,2,1,0:T(8,128)}, f32[2,64,1024]{2,1,0:T(8,128)}, f32[64,1024]{1,0:T(8,128)}) custom-call(s32[256]{0:T(256)} %col_ref.1, f32[19,64,1024]{2,1,0:T(8,128)} %bitcast.8, f32[2,64,1024]{2,1,0:T(8,128)} %bitcast.9, f32[64,1024]{1,0:T(8,128)} %bitcast.10, f32[64,1024]{1,0:T(8,128)} %bitcast.11, s32[64,1024]{1,0:T(8,128)} %bitcast.12), custom_call_target="tpu_custom_call" | custom-call | flops 100000000 | bytes 12000000 | tf_op jit(solution)/shard_map/pallas_call | solution.py:886
  83.4 5.5 %shard_map.86 = (f32[19,64,1024]{2,1,0:T(8,128)}, f32[2,64,1024]{2,1,0:T(8,128)}, f32[64,1024]{1,0:T(8,128)}) custom-call(f32[19,10,96,128]{3,2,1,0:T(8,128)} %get-tuple-element.9.g_hbm, f32[2,64,1024]{2,1,0:T(8,128)} %get-tuple-element.10.conc_hbm, f32[64,1024]{1,0:T(8,128)} %get-tuple-element.11.pot_hbm), custom_call_target="tpu_custom_call" | custom-call | flops 10000000 | bytes 12000000 | tf_op jit(solution)/shard_map/pallas_call | solution.py:910
